TPU v7x, 1024 devices: a whole 4x8x16 slice. The times are simulated.
1024 devices in a mesh: users: 64 (over x, z), items: 16 (over y, core).
Axes of the slice: x: 4, y: 8, z: 16, core: 2. Of those that a mesh axis runs over, the one named last changes fastest.
Arguments:
- user_factors: bfloat16 [16384, 256], P('users'), may hold values from -1.5 to 1.5
- item_factors: bfloat16 [32768, 256], P('items'), may hold values from -1.5 to 1.5
- pattern: int32 [128, 16, 16], P('users', 'items'), may hold values from 0 to 15
- counts: int32 [128, 16], P('users', 'items'), may hold values from 1 to 16, as said below
- confidence: bfloat16 [128, 16, 16, 128, 128], P('users', 'items'), may hold values from 0 to 16, as said below
Outputs:
- user_gradient: float32 [16384, 256], P(('users', 'items'))
- item_gradient: float32 [16, 2048, 256], P('items', 'users')
Inputs may be any that keep to these rules, and one draw needn't show every extreme that they name: `counts`: every user tile has 16 live slots in one item shard. `confidence`: about half of the entries are zero.
All inputs are finite; a program needn't handle non-finite values.
Results may differ from a plain program's by a relative error of at most 0.00098.
Values sent between devices are 32-bit elements; how exact they have to be, the bound alone decides.
No kernel may reach another device: no remote copies, remote signals or barrier semaphores. Data moves between devices by JAX's collectives and lax.ppermute only.
A program may use at most 32 MiB of HBM per device.

v0:
```python
import math

import jax
import jax.numpy as jnp
from jax import lax
from jax.sharding import PartitionSpec as P

WEIGHT_ALL = 8.0
RIDGE_COEF = 0.5


def shards(user_factors, item_factors, pattern, counts, confidence):
    highest = lax.Precision.HIGHEST
    user_size = lax.axis_size("users")
    item_size = lax.axis_size("items")
    user_index = lax.axis_index("users")
    item_index = lax.axis_index("items")
    user_rows, feat_width = user_factors.shape
    item_rows = item_factors.shape[0]
    tile_rows = confidence.shape[-1]
    slot_count = pattern.shape[-1]
    user_tiles = user_rows // tile_rows
    item_tiles = item_rows // tile_rows
    users_total = user_rows * user_size
    items_total = item_rows * item_size
    share_rows = user_rows // item_size
    owner_rows = item_rows // user_size
    own_user = lax.dynamic_slice_in_dim(user_factors, item_index * share_rows, share_rows, 0)
    own_item = lax.dynamic_slice_in_dim(item_factors, user_index * owner_rows, owner_rows, 0)
    gram_x = lax.psum(
        jnp.dot(user_factors.T, user_factors, preferred_element_type=jnp.float32), "users"
    )
    gram_y = lax.psum(
        jnp.dot(item_factors.T, item_factors, preferred_element_type=jnp.float32), "items"
    )
    user_blocks = user_factors.reshape(user_tiles, tile_rows, feat_width)
    item_blocks = item_factors.reshape(item_tiles, tile_rows, feat_width)
    chosen = pattern[:, 0, :]
    gathered = item_blocks[chosen]
    scores = jnp.einsum("bak,bsck->bsac", user_blocks, gathered, preferred_element_type=jnp.float32)
    slot_ids = lax.broadcasted_iota(jnp.int32, (user_tiles, slot_count), 1)
    valid_mask = (slot_ids < counts).astype(jnp.float32)
    residual_tiles = (
        valid_mask[:, :, None, None] * confidence[:, 0].astype(jnp.float32) * (scores - 1.0)
    ).astype(jnp.bfloat16)
    user_part = jnp.einsum(
        "bsac,bsck->bak", residual_tiles, gathered, preferred_element_type=jnp.float32
    ).reshape(user_rows, feat_width)
    user_share = lax.psum_scatter(user_part, "items", scatter_dimension=0, tiled=True)
    norm_user = math.sqrt(slot_count * item_size * tile_rows)
    own_user_f = own_user.astype(jnp.float32)
    user_gradient = 2.0 * (
        WEIGHT_ALL * jnp.dot(own_user_f, gram_y, precision=highest) / items_total
        + user_share / norm_user
        + RIDGE_COEF * own_user_f
    )
    contrib = jnp.einsum(
        "bsac,bak->bsck", residual_tiles, user_blocks, preferred_element_type=jnp.float32
    )
    contrib = contrib.reshape(user_tiles * slot_count, tile_rows * feat_width)
    flat_chosen = chosen.reshape(-1)
    tile_ids = lax.broadcasted_iota(jnp.int32, (1, item_tiles), 1)
    select = (flat_chosen[:, None] == tile_ids).astype(jnp.float32)
    partial_sum = jnp.dot(select.T, contrib, precision=highest).reshape(item_rows, feat_width)
    item_share = lax.psum_scatter(partial_sum, "users", scatter_dimension=0, tiled=True)
    norm_item = math.sqrt(users_total * slot_count / item_tiles)
    own_item_f = own_item.astype(jnp.float32)
    item_gradient = 2.0 * (
        WEIGHT_ALL * jnp.dot(own_item_f, gram_x, precision=highest) / users_total
        + item_share / norm_item
        + RIDGE_COEF * own_item_f
    )
    return (user_gradient, item_gradient[None])


def solution(mesh):
    placed = (
        P("users", None),
        P("items", None),
        P("users", "items", None),
        P("users", "items"),
        P("users", "items", None, None, None),
    )
    return jax.shard_map(
        shards,
        mesh=mesh,
        in_specs=placed,
        out_specs=(P(("users", "items"), None), P("items", "users", None)),
        check_vma=False,
    )
```

profile of v0, /device:TPU:56, one launch (start us, length us, event | category | flops | bytes accessed | tf_op | source)
XLA Modules:
  0.0 1199.5 jit_solution(10591931242849001301)
XLA Ops:
  7.2 0.0 all-reduce.3.cloned.1.call-start
  7.3 2.9 fusion.15
  10.1 0.0 all-reduce.3.cloned.1.call-update
  10.1 0.0 reduce-scatter.3.cloned.1.call-start
  10.2 0.1 reshape.79
  10.3 0.0 copy-done.3
  10.3 1.3 copy.7
  11.6 0.0 copy-done.5
  11.6 0.1 compare_convert_fusion
  11.7 0.7 gather_fusion
  12.4 0.2 copy-done.2
  12.6 1.9 fusion.1
  14.5 1.3 fusion.16
  15.8 0.0 reduce-scatter.3.cloned.1.call-update
  15.8 0.0 all-reduce.5.cloned.1.call-start
  15.9 0.9 fusion.17
  16.8 0.0 all-reduce.5.cloned.1.call-update
  16.8 0.0 reduce-scatter.5.cloned.1.call-start
  16.9 1.9 fusion.18
  18.8 4.4 copy.12
  23.2 0.5 broadcast.46
  23.7 0.7 reduce.3
  24.4 0.1 eq.15
  24.4 3.4 fusion.10
  27.8 1.5 reshape.75
  29.3 0.0 reduce-scatter.5.cloned.1.call-update
  29.4 112.5 %all-reduce.3.cloned.1.call-done = f32[256,256]{1,0:T(8,128)} async-done(((f32[256,256]{1,0:T(8,128)}), f32[256,256]{1,0:T(8,128)}) %all-reduce.3.cloned.1.call-update) | async-done | bytes 262160 | tf_op jit(solution)/shard_map/psum | solution.py:33
  141.8 65.9 %reduce-scatter.3.cloned.1.call-done = f32[16,256]{1,0:T(8,128)} async-done(((f32[256,256]{1,0:T(8,128)}), f32[16,256]{1,0:T(8,128)}) %reduce-scatter.3.cloned.1.call-update) | async-done | bytes 16400 | tf_op jit(solution)/shard_map/reduce_scatter | solution.py:49
  207.7 1.8 fusion.8
  209.5 280.2 %all-reduce.5.cloned.1.call-done = f32[256,256]{1,0:T(8,128)} async-done(((f32[256,256]{1,0:T(8,128)}), f32[256,256]{1,0:T(8,128)}) %all-reduce.5.cloned.1.call-update) | async-done | bytes 262160 | tf_op jit(solution)/shard_map/psum | solution.py:30
  489.7 701.5 %reduce-scatter.5.cloned.1.call-done = f32[32,256]{1,0:T(8,128)} async-done(((f32[2048,256]{1,0:T(8,128)}), f32[32,256]{1,0:T(8,128)}) %reduce-scatter.5.cloned.1.call-update) | async-done | bytes 32784 | tf_op jit(solution)/shard_map/reduce_scatter | solution.py:65
  1191.1 1.8 fusion.5
  (11 shorter events, 0.0 us)
Async XLA Ops:
  7.2 4.5 copy-start
  7.2 3.0 copy-start.4
  7.2 3.1 copy-start.3
  7.2 4.4 copy-start.5
  7.2 134.6 %all-reduce.3.cloned.1.call-start = ((), (), s32[]{:S(2)}) async-start(), calls=%async_computation.2 | async-start | bytes 524288 | tf_op jit(solution)/shard_map/psum | solution.py:33
  10.1 197.5 %reduce-scatter.3.cloned.1.call-start = ((), (), s32[]{:S(2)}) async-start(), calls=%async_computation.3 | async-start | bytes 278528 | tf_op jit(solution)/shard_map/reduce_scatter | solution.py:49
  11.7 0.9 copy-start.2
  14.5 1.3 copy-start.1
  15.8 473.9 %all-reduce.5.cloned.1.call-start = ((), (), s32[]{:S(2)}) async-start(), calls=%async_computation.4 | async-start | bytes 524288 | tf_op jit(solution)/shard_map/psum | solution.py:30
  16.8 1174.3 %reduce-scatter.5.cloned.1.call-start = ((), (), s32[]{:S(2)}) async-start(), calls=%async_computation.5 | async-start | bytes 2129920 | tf_op jit(solution)/shard_map/reduce_scatter | solution.py:65
Sparse Core Ops, SparseCore 0:
  10.4 131.4 all-reduce.2
  145.6 62.0 reduce-scatter.2
  211.1 278.5 all-reduce.4
  496.0 695.0 reduce-scatter.4
where the time goes:
time: 1200 us
  waiting for transfers between devices  1160 us (97%)
  matrix products  15.9 us (1%)
  between operations  13.9 us (1%)
    reduce_scatter x1, waiting for transfers between devices, shards(): lax.psum_scatter(partial_sum, 'users', scatter_dimension=0, tiled=True)  701 us
    psum x1, waiting for transfers between devices, shards(): lax.psum(jnp.dot(user_factors.T, user_factors, preferred_element_type=jnp...  280 us
    psum x1, waiting for transfers between devices, shards(): lax.psum(jnp.dot(item_factors.T, item_factors, preferred_element_type=jnp...  112 us
    reduce_scatter x1, waiting for transfers between devices, shards(): lax.psum_scatter(user_part, 'items', scatter_dimension=0, tiled=True)  65.9 us
  transfers between devices with their start and end apart: 4, of which 4 were waited for; matrix products, arithmetic and copies ran while one was open for 2% of the time, Pallas kernels for 0%

commit v1 on v0

v1 whole, which is shorter than its diff:
```python
import math

import jax
import jax.numpy as jnp
from jax import lax
from jax.experimental import pallas as pl
from jax.experimental.pallas import tpu as pltpu
from jax.sharding import Mesh, PartitionSpec as P

WEIGHT_ALL = 8.0
RIDGE_COEF = 0.5
F32 = jnp.float32
BF16 = jnp.bfloat16


def dot(a, b, dims):
    return lax.dot_general(a, b, (dims, ((), ())), preferred_element_type=F32)


def split(a):
    high = a.astype(BF16)
    return high, (a - high.astype(F32)).astype(BF16)


def local_kernel(item_scale, item_gram, user_scale, user_gram,
                 pat, cnt, x_ref, y_ref, c_ref, item_ref, user_ref, s_ref, w_ref):
    user_tiles, slots, tile, _ = c_ref.shape
    item_tiles = y_ref.shape[0] // tile
    x = x_ref[...]
    for t in range(item_tiles):
        y_t = y_ref[t * tile:(t + 1) * tile, :]
        s_ref[t] = dot(x, y_t, ((1,), (1,))) - 1.0
        w_ref[t] = jnp.zeros_like(w_ref[t])
    for b in range(user_tiles):
        rows = pl.ds(b * tile, tile)
        for s in range(slots):
            @pl.when(s < cnt[b, 0])
            def _():
                t = pat[b, s]
                residual = (c_ref[b, s].astype(F32) * s_ref[t, rows, :]).astype(BF16)
                w_ref[t, rows, :] += residual.astype(F32)
    gx_high, gx_low = split(dot(x, x, ((0,), (0,))) * item_gram)
    y = y_ref[...]
    gy_high, gy_low = split(dot(y, y, ((0,), (0,))) * user_gram)
    user = jnp.zeros(user_ref.shape, F32)
    for t in range(item_tiles):
        y_t = y_ref[t * tile:(t + 1) * tile, :]
        high, low = split(w_ref[t])
        user += dot(high, y_t, ((1,), (0,))) + dot(low, y_t, ((1,), (0,)))
        part = dot(high, x, ((0,), (0,))) + dot(low, x, ((0,), (0,)))
        gram = dot(y_t, gx_high, ((1,), (0,))) + dot(y_t, gx_low, ((1,), (0,)))
        item_ref[t * tile:(t + 1) * tile, :] = part * item_scale + gram
    gram = dot(x, gy_high, ((1,), (0,))) + dot(x, gy_low, ((1,), (0,)))
    user_ref[...] = user * user_scale + gram


def shards(user_factors, item_factors, pattern, counts, confidence):
    user_size = lax.axis_size(("x", "z"))
    item_size = lax.axis_size(("y", "core"))
    user_index = lax.axis_index(("x", "z"))
    item_index = lax.axis_index(("y", "core"))
    user_rows, feat_width = user_factors.shape
    item_rows = item_factors.shape[0]
    tile_rows = confidence.shape[-1]
    slot_count = pattern.shape[-1]
    user_tiles = user_rows // tile_rows
    item_tiles = item_rows // tile_rows
    users_total = user_rows * user_size
    items_total = item_rows * item_size
    share_rows = user_rows // item_size
    owner_rows = item_rows // user_size
    norm_user = math.sqrt(slot_count * item_size * tile_rows)
    norm_item = math.sqrt(users_total * slot_count / item_tiles)

    item_part, user_part = pl.pallas_call(
        lambda *refs: local_kernel(
            2.0 / norm_item, 2.0 * WEIGHT_ALL / users_total,
            2.0 / norm_user, 2.0 * WEIGHT_ALL / items_total, *refs),
        out_shape=(
            jax.ShapeDtypeStruct((item_rows, feat_width), F32),
            jax.ShapeDtypeStruct((user_rows, feat_width), F32),
        ),
        in_specs=[
            pl.BlockSpec(memory_space=pltpu.SMEM),
            pl.BlockSpec(memory_space=pltpu.SMEM),
            pl.BlockSpec(memory_space=pltpu.VMEM),
            pl.BlockSpec(memory_space=pltpu.VMEM),
            pl.BlockSpec(memory_space=pltpu.VMEM),
        ],
        out_specs=(
            pl.BlockSpec(memory_space=pltpu.VMEM),
            pl.BlockSpec(memory_space=pltpu.VMEM),
        ),
        scratch_shapes=[
            pltpu.VMEM((item_tiles, user_rows, tile_rows), F32),
            pltpu.VMEM((item_tiles, user_rows, tile_rows), F32),
        ],
        compiler_params=pltpu.CompilerParams(vmem_limit_bytes=32 * 1024 * 1024),
        name="local_sums",
    )(pattern[:, 0, :], counts, user_factors, item_factors, confidence[:, 0])

    def reduce_over(part, axes):
        size = lax.axis_size(axes)
        moved = lax.all_to_all(part, axes, 0, 0, tiled=True)
        return moved.reshape(size, part.shape[0] // size, feat_width).sum(0)

    item_x = reduce_over(item_part, "x")
    user_share = reduce_over(user_part, ("y", "core"))
    item_share = reduce_over(item_x, "z")

    own_user = lax.dynamic_slice_in_dim(user_factors, item_index * share_rows, share_rows, 0)
    own_item = lax.dynamic_slice_in_dim(item_factors, user_index * owner_rows, owner_rows, 0)
    user_gradient = user_share + 2.0 * RIDGE_COEF * own_user.astype(F32)
    item_gradient = item_share + 2.0 * RIDGE_COEF * own_item.astype(F32)
    return (user_gradient, item_gradient[None])


def solution(mesh):
    fine = Mesh(mesh.devices.reshape(4, 16, 8, 2), ("x", "z", "y", "core"))
    users, items = ("x", "z"), ("y", "core")
    return jax.shard_map(
        shards,
        mesh=fine,
        in_specs=(
            P(users, None),
            P(items, None),
            P(users, items, None),
            P(users, items),
            P(users, items, None, None, None),
        ),
        out_specs=(P(users + items, None), P(items, users, None)),
        check_vma=False,
    )
```

time: 1200 us -> 110 us (0.09)
  the two profiles are of different devices: /device:TPU:56 before, /device:TPU:64 now
where the time goes in v1:
time: 110 us; the launch traced here: 109 us
  waiting for transfers between devices  38.6 us (35%)
  blocking collectives  30.4 us (28%)
  starting transfers between devices  25.7 us (23%)
  Pallas kernels  5.28 us (5%)
  local copies, waits for them, and re-layouts  4.77 us (4%)
  other arithmetic  3.66 us (3%)
    all_to_all x2, waiting for transfers between devices, reduce_over(): moved = lax.all_to_all(part, axes, 0, 0, tiled=True)  38.6 us
    all_to_all x1, blocking collectives, reduce_over(): moved = lax.all_to_all(part, axes, 0, 0, tiled=True)  30.4 us
    all_to_all x2, starting transfers between devices, reduce_over(): moved = lax.all_to_all(part, axes, 0, 0, tiled=True)  25.7 us
    pallas_call x1, Pallas kernels, shards(): pl.pallas_call(lambda *refs: local_kernel(2.0 / norm_item, 2.0 * WEIGHT_A...  5.28 us
    unnamed x9, local copies, waits for them, and re-layouts  4.77 us
  transfers between devices with their start and end apart: 2, of which 2 were waited for; matrix products, arithmetic and copies ran while one was open for 2% of the time, Pallas kernels for 0%

profile of v1, /device:TPU:64, one launch (start us, length us, event | category | flops | bytes accessed | tf_op | source)
XLA Modules:
  0.0 109.1 jit_solution(16955132004182528601)
XLA Ops:
  0.6 0.7 copy.8.refs_1_
  1.4 0.0 copy-start
  1.4 1.2 %copy-done = bf16[2048,256]{1,0:T(8,128)(2,1)S(1)} copy-done((bf16[2048,256]{1,0:T(8,128)(2,1)S(1)}, bf16[2048,256]{1,0:T(8,128)(2,1)}, u32[]{:S(2)}) %copy-start) | copy-done | bytes 1048600
  2.6 0.0 copy-start.1
  2.6 1.2 %copy-done.1 = bf16[2,1,16,128,128]{4,3,2,1,0:T(8,128)(2,1)S(1)} copy-done((bf16[2,1,16,128,128]{4,3,2,1,0:T(8,128)(2,1)S(1)}, bf16[2,1,16,128,128]{4,3,2,1,0:T(8,128)(2,1)}, u32[]{:S(2)}) %copy-start.1) | copy-done | bytes 1048600
  3.8 0.0 copy-start.2
  3.8 0.9 copy-done.2
  4.7 0.0 copy-start.3
  4.7 0.7 copy-done.3
  5.4 5.3 %local_sums.1 = (f32[2048,256]{1,0:T(8,128)S(1)}, f32[256,256]{1,0:T(8,128)}) custom-call(s32[2,16]{1,0:T(2,128)S(1)} %bitcast.9, s32[2,1]{1,0:T(2,128)S(1)} %copy.8.refs_1_, bf16[256,256]{1,0:T(8,128)(2,1)S(1)} %copy-done.2, bf16[2048,256]{1,0:T(8,128)(2,1)S(1)} %copy-done, bf16[2,16,128,128]{3,2,1,0:T(8,128)(2,1)S(1)} %bitcast.8), custom_call_target="tpu_custom_call" | custom-call | tf_op jit(solution)/shard_map/local_sums/pallas_call | solution.py:75
  10.7 30.4 %all_to_all.27 = f32[4,512,256]{2,1,0:T(8,128)S(1)} all-to-all(f32[4,512,256]{2,1,0:T(8,128)S(1)} %bitcast.7), channel_id=1, replica_groups=mesh['x'=4,'z'=16,'y'=8,'core'=2] {'x'}, dimensions={0} | all-to-all | bytes 4194304 | tf_op jit(solution)/shard_map/all_to_all | solution.py:104
  41.1 7.4 %all-to-all-start = ((f32[16,16,256]{2,1,0:T(8,128)}), f32[16,16,256]{2,1,0:T(8,128)S(1)}, u32[]{:S(2)}, u32[]{:S(2)}) async-start(f32[16,16,256]{2,1,0:T(8,128)} %bitcast.2), calls=%async_computation | async-start | bytes 524288 | tf_op jit(solution)/shard_map/all_to_all | solution.py:104
  48.5 0.9 reduce_sum.28
  49.4 10.2 %all-to-all-done = f32[16,16,256]{2,1,0:T(8,128)S(1)} async-done(((f32[16,16,256]{2,1,0:T(8,128)}), f32[16,16,256]{2,1,0:T(8,128)S(1)}, u32[]{:S(2)}, u32[]{:S(2)}) %all-to-all-start) | async-done | bytes 262176 | tf_op jit(solution)/shard_map/all_to_all | solution.py:104
  59.7 18.4 %all-to-all-start.2 = ((f32[16,32,256]{2,1,0:T(8,128)}), f32[16,32,256]{2,1,0:T(8,128)S(1)}, u32[]{:S(2)}, u32[]{:S(2)}) async-start(f32[16,32,256]{2,1,0:T(8,128)} %bitcast.4), calls=%async_computation.2 | async-start | bytes 1048576 | tf_op jit(solution)/shard_map/all_to_all | solution.py:104
  78.0 1.3 %convert_add_fusion = f32[16,256]{1,0:T(8,128)} fusion(f32[16,256]{1,0:T(8,128)S(1)} %reduce_sum.27, bf16[256,256]{1,0:T(8,128)(2,1)} %refs_2_.1, s32[]{:T(128)S(6)} %select_n.6), kind=kLoop, calls=%fused_computation.1 | loop fusion | flops 8192 | bytes 40964 | tf_op jit(solution)/shard_map/add | solution.py:113
  79.4 28.3 %all-to-all-done.2 = f32[16,32,256]{2,1,0:T(8,128)S(1)} async-done(((f32[16,32,256]{2,1,0:T(8,128)}), f32[16,32,256]{2,1,0:T(8,128)S(1)}, u32[]{:S(2)}, u32[]{:S(2)}) %all-to-all-start.2) | async-done | bytes 524320 | tf_op jit(solution)/shard_map/all_to_all | solution.py:104
  107.7 1.3 %add_bitcast_fusion = f32[1,32,256]{2,1,0:T(8,128)} fusion(f32[32,256]{1,0:T(8,128)S(1)} %reduce_sum.29, bf16[2048,256]{1,0:T(8,128)(2,1)} %refs_3_.1, s32[]{:T(128)S(6)} %select_n.7), kind=kLoop, calls=%fused_computation | loop fusion | flops 16384 | bytes 81924 | tf_op jit(solution)/shard_map/broadcast_in_dim | solution.py:115
  (2 shorter events, 0.1 us)
Async XLA Ops:
  1.4 1.2 %copy-start = (bf16[2048,256]{1,0:T(8,128)(2,1)S(1)}, bf16[2048,256]{1,0:T(8,128)(2,1)}, u32[]{:S(2)}) copy-start(bf16[2048,256]{1,0:T(8,128)(2,1)} %refs_3_.1) | copy-start | bytes 3145732
  2.6 1.2 %copy-start.1 = (bf16[2,1,16,128,128]{4,3,2,1,0:T(8,128)(2,1)S(1)}, bf16[2,1,16,128,128]{4,3,2,1,0:T(8,128)(2,1)}, u32[]{:S(2)}) copy-start(bf16[2,1,16,128,128]{4,3,2,1,0:T(8,128)(2,1)} %param.9) | copy-start | bytes 3145732
  3.8 0.9 copy-start.2
  4.7 0.7 copy-start.3
  41.1 18.6 %all-to-all-start = ((f32[16,16,256]{2,1,0:T(8,128)}), f32[16,16,256]{2,1,0:T(8,128)S(1)}, u32[]{:S(2)}, u32[]{:S(2)}) async-start(f32[16,16,256]{2,1,0:T(8,128)} %bitcast.2), calls=%async_computation | async-start | bytes 524288 | tf_op jit(solution)/shard_map/all_to_all | solution.py:104
  59.7 48.0 %all-to-all-start.2 = ((f32[16,32,256]{2,1,0:T(8,128)}), f32[16,32,256]{2,1,0:T(8,128)S(1)}, u32[]{:S(2)}, u32[]{:S(2)}) async-start(f32[16,32,256]{2,1,0:T(8,128)} %bitcast.4), calls=%async_computation.2 | async-start | bytes 1048576 | tf_op jit(solution)/shard_map/all_to_all | solution.py:104

commit v2 on v1

v2 whole, which is shorter than its diff:
```python
import math

import jax
import jax.numpy as jnp
from jax import lax
from jax.experimental import pallas as pl
from jax.experimental.pallas import tpu as pltpu
from jax.sharding import Mesh, PartitionSpec as P

WEIGHT_ALL = 8.0
RIDGE_COEF = 0.5
F32 = jnp.float32
BF16 = jnp.bfloat16
USERS = ("x", "zh", "zl")
ITEMS = ("y", "core")


def dot(a, b, dims):
    return lax.dot_general(a, b, (dims, ((), ())), preferred_element_type=F32)


def split(a):
    high = a.astype(BF16)
    return high, (a - high.astype(F32)).astype(BF16)


def eye(n, value):
    row = lax.broadcasted_iota(jnp.int32, (n, n), 0)
    col = lax.broadcasted_iota(jnp.int32, (n, n), 1)
    return jnp.where(row == col, value, 0.0).astype(F32)


def local_kernel(scales, sizes, x_hbm, y_hbm, c_hbm, pat_hbm, cnt_hbm, item_ref, user_ref,
                 x_ref, y_ref, c_ref, pat, cnt, s_ref, w_ref, sems):
    item_scale, item_gram, item_ridge, user_scale, user_gram, user_ridge = scales
    x_size, zh_size, zl_size = sizes
    user_tiles, _, slots, tile, _ = c_ref.shape
    width = x_ref.shape[1]
    item_rows = y_ref.shape[0]
    item_tiles = item_rows // tile
    owner_rows = item_rows // (x_size * zh_size * zl_size)
    block = min(tile, owner_rows)
    copies = [
        pltpu.make_async_copy(src, dst, sems.at[k])
        for k, (src, dst) in enumerate(
            ((x_hbm, x_ref), (y_hbm, y_ref), (pat_hbm, pat), (cnt_hbm, cnt), (c_hbm, c_ref)))
    ]
    for copy in copies:
        copy.start()
    w_ref[...] = jnp.zeros_like(w_ref)
    copies[0].wait()
    copies[1].wait()
    x = x_ref[...]
    for t in range(item_tiles):
        s_ref[t] = dot(x, y_ref[t * tile:(t + 1) * tile, :], ((1,), (1,))) - 1.0
    for copy in copies[2:]:
        copy.wait()
    for b in range(user_tiles):
        rows = pl.ds(b * tile, tile)
        for s in range(slots):
            t = pat[b, 0, s]
            live = jnp.where(s < cnt[0, b], 1.0, 0.0).astype(F32)
            residual = (live * c_ref[b, 0, s].astype(F32) * s_ref[t, rows, :]).astype(BF16)
            w_ref[t, rows, :] += residual.astype(F32)
    gx_high, gx_low = split(dot(x, x, ((0,), (0,))) * item_gram + eye(width, item_ridge))
    y = y_ref[...]
    gy_high, gy_low = split(dot(y, y, ((0,), (0,))) * user_gram + eye(width, user_ridge))
    user = jnp.zeros(user_ref.shape, F32)
    for t in range(item_tiles):
        y_t = y_ref[t * tile:(t + 1) * tile, :]
        high, low = split(w_ref[t])
        user += dot(high, y_t, ((1,), (0,))) + dot(low, y_t, ((1,), (0,)))
        part = dot(high, x, ((0,), (0,))) + dot(low, x, ((0,), (0,)))
        gram = dot(y_t, gx_high, ((1,), (0,))) + dot(y_t, gx_low, ((1,), (0,)))
        whole = part * item_scale + gram
        for k in range(0, tile, block):
            owner, offset = divmod(t * tile + k, owner_rows)
            xi, zh, zl = owner // (zh_size * zl_size), owner // zl_size % zh_size, owner % zl_size
            place = ((xi * zl_size + zl) * zh_size + zh) * owner_rows + offset
            item_ref[place:place + block, :] = whole[k:k + block, :]
    gram = dot(x, gy_high, ((1,), (0,))) + dot(x, gy_low, ((1,), (0,)))
    user_ref[...] = user * user_scale + gram


def shards(user_factors, item_factors, pattern, counts, confidence):
    user_size = lax.axis_size(USERS)
    item_size = lax.axis_size(ITEMS)
    user_rows, feat_width = user_factors.shape
    item_rows = item_factors.shape[0]
    tile_rows = confidence.shape[-1]
    slot_count = pattern.shape[-1]
    user_tiles = user_rows // tile_rows
    item_tiles = item_rows // tile_rows
    users_total = user_rows * user_size
    items_total = item_rows * item_size
    norm_user = math.sqrt(slot_count * item_size * tile_rows)
    norm_item = math.sqrt(users_total * slot_count / item_tiles)
    scales = (
        2.0 / norm_item, 2.0 * WEIGHT_ALL / users_total, 2.0 * RIDGE_COEF / user_size,
        2.0 / norm_user, 2.0 * WEIGHT_ALL / items_total, 2.0 * RIDGE_COEF / item_size,
    )
    sizes = tuple(lax.axis_size(name) for name in USERS)

    item_part, user_part = pl.pallas_call(
        lambda *refs: local_kernel(scales, sizes, *refs),
        out_shape=(
            jax.ShapeDtypeStruct((item_rows, feat_width), F32),
            jax.ShapeDtypeStruct((user_rows, feat_width), F32),
        ),
        in_specs=[pl.BlockSpec(memory_space=pltpu.HBM)] * 5,
        out_specs=(
            pl.BlockSpec(memory_space=pltpu.VMEM),
            pl.BlockSpec(memory_space=pltpu.VMEM),
        ),
        scratch_shapes=[
            pltpu.VMEM(user_factors.shape, BF16),
            pltpu.VMEM(item_factors.shape, BF16),
            pltpu.VMEM(confidence.shape, BF16),
            pltpu.SMEM(pattern.shape, jnp.int32),
            pltpu.SMEM((1, user_tiles), jnp.int32),
            pltpu.VMEM((item_tiles, user_rows, tile_rows), F32),
            pltpu.VMEM((item_tiles, user_rows, tile_rows), F32),
            pltpu.SemaphoreType.DMA((5,)),
        ],
        compiler_params=pltpu.CompilerParams(vmem_limit_bytes=60 * 1024 * 1024),
        name="local_sums",
    )(user_factors, item_factors, confidence, pattern, counts.T)

    def reduce_over(part, axes):
        size = lax.axis_size(axes)
        moved = lax.all_to_all(part, axes, 0, 0, tiled=True)
        return moved.reshape(size, part.shape[0] // size, feat_width).sum(0)

    item_half = reduce_over(item_part, ("x", "zl"))
    item_gradient = reduce_over(item_half, "zh")

    user_pair = lax.psum_scatter(user_part, "y", scatter_dimension=0, tiled=True)
    cores = lax.axis_size("core")
    share_rows = user_pair.shape[0] // cores
    core = lax.axis_index("core")
    mine = lax.dynamic_slice_in_dim(user_pair, core * share_rows, share_rows, 0)
    if cores == 1:
        user_gradient = mine
    else:
        other = lax.dynamic_slice_in_dim(user_pair, (1 - core) * share_rows, share_rows, 0)
        user_gradient = mine + lax.ppermute(other, "core", [(0, 1), (1, 0)])
    return (user_gradient, item_gradient[None])


def solution(mesh):
    fine = Mesh(mesh.devices.reshape(4, 8, 2, 8, 2), USERS + ITEMS)
    return jax.shard_map(
        shards,
        mesh=fine,
        in_specs=(
            P(USERS, None),
            P(ITEMS, None),
            P(USERS, ITEMS, None),
            P(USERS, ITEMS),
            P(USERS, ITEMS, None, None, None),
        ),
        out_specs=(P(USERS + ITEMS, None), P(ITEMS, USERS, None)),
        check_vma=False,
    )
```

time: 110 us -> 127 us (1.15)
  the two profiles are of different devices: /device:TPU:64 before, /device:TPU:56 now
where the time goes in v2:
time: 127 us; the launch traced here: 125 us
  waiting for transfers between devices  48.2 us (38%)
  blocking collectives  33.4 us (26%)
  starting transfers between devices  19.8 us (16%)
  between operations  14.1 us (11%)
  Pallas kernels  6.36 us (5%)
  other arithmetic  2.79 us (2%)
    reduce_scatter x1, waiting for transfers between devices, shards(): lax.psum_scatter(user_part, 'y', scatter_dimension=0, tiled=True)  46.4 us
    all_to_all x1, blocking collectives, reduce_over(): moved = lax.all_to_all(part, axes, 0, 0, tiled=True)  33.4 us
    all_to_all x1, starting transfers between devices, reduce_over(): moved = lax.all_to_all(part, axes, 0, 0, tiled=True)  17.9 us
    pallas_call x1, Pallas kernels, shards(): pl.pallas_call(lambda *refs: local_kernel(scales, sizes, *refs), out_shap...  6.36 us
  transfers between devices with their start and end apart: 3, of which 2 were waited for; matrix products, arithmetic and copies ran while one was open for 2% of the time, Pallas kernels for 0%

profile of v2, /device:TPU:56, one launch (start us, length us, event | category | flops | bytes accessed | tf_op | source)
XLA Modules:
  0.0 125.3 jit_solution(13398832248072195578)
XLA Ops:
  7.2 6.4 %local_sums.1 = (f32[2048,256]{1,0:T(8,128)}, f32[256,256]{1,0:T(8,128)}) custom-call(bf16[256,256]{1,0:T(8,128)(2,1)} %refs_0_.1, bf16[2048,256]{1,0:T(8,128)(2,1)} %refs_1_.1, bf16[2,1,16,128,128]{4,3,2,1,0:T(8,128)(2,1)} %refs_2_.1, s32[2,1,16]{2,1,0:T(1,128)} %refs_3_.1, s32[1,2]{1,0:T(1,128)} %bitcast.6), custom_call_target="tpu_custom_call" | custom-call | tf_op jit(solution)/shard_map/local_sums/pallas_call | solution.py:104
  13.5 33.4 %all_to_all.18 = f32[8,256,256]{2,1,0:T(8,128)S(1)} all-to-all(f32[8,256,256]{2,1,0:T(8,128)} %bitcast.4), channel_id=1, replica_groups=mesh['x'=4,'zh'=8,'zl'=2,'y'=8,'core'=2] {'x','zl'}, dimensions={0} | all-to-all | bytes 4194304 | tf_op jit(solution)/shard_map/all_to_all | solution.py:131
  46.9 0.8 reduce_sum.18
  47.7 17.9 %all-to-all-start.1 = ((f32[8,32,256]{2,1,0:T(8,128)}), f32[8,32,256]{2,1,0:T(8,128)S(1)}, u32[]{:S(2)}, u32[]{:S(2)}) async-start(f32[8,32,256]{2,1,0:T(8,128)} %bitcast.2), calls=%async_computation.2 | async-start | bytes 524288 | tf_op jit(solution)/shard_map/all_to_all | solution.py:131
  65.6 0.0 reduce-scatter.2.cloned.1.call-start
  65.6 0.7 reduce-scatter.2.cloned.1.call-update
  66.3 46.4 %reduce-scatter.2.cloned.1.call-done = f32[32,256]{1,0:T(8,128)} async-done(((f32[256,256]{1,0:T(8,128)}), f32[32,256]{1,0:T(8,128)}) %reduce-scatter.2.cloned.1.call-update) | async-done | bytes 32784 | tf_op jit(solution)/shard_map/reduce_scatter | solution.py:137
  112.7 0.7 constant_dynamic-slice_fusion
  113.4 1.9 %collective-permute-start = (f32[16,256]{1,0:T(8,128)S(1)}, f32[16,256]{1,0:T(8,128)S(1)}, u32[]{:S(2)}, u32[]{:S(2)}) collective-permute-start(f32[16,256]{1,0:T(8,128)S(1)} %constant_dynamic-slice_fusion), channel_id=1, source_target_pairs={{0,1},{1,0},{2,3},{3,2},{4,5},{5,4},{6,7},{7,6},{8,9},{9,8},{10,11... | collective-permute-start | bytes 49160 | tf_op jit(solution)/shard_map/ppermute | solution.py:146
  115.4 1.1 collective-permute-done
  116.5 1.3 %dynamic-slice_add_fusion = f32[16,256]{1,0:T(8,128)} fusion(f32[16,256]{1,0:T(8,128)S(1)} %collective-permute-done, f32[32,256]{1,0:T(8,128)} %reduce-scatter.2.cloned.1.call-done, s32[]{:T(128)S(6)} %select_n.6), kind=kLoop, calls=%fused_computation | loop fusion | flops 4096 | bytes 49156 | tf_op jit(solution)/shard_map/add | solution.py:146
  117.8 0.0 all-to-all-done.1
  117.8 0.6 reduce_sum.19
Async XLA Ops:
  47.7 70.1 %all-to-all-start.1 = ((f32[8,32,256]{2,1,0:T(8,128)}), f32[8,32,256]{2,1,0:T(8,128)S(1)}, u32[]{:S(2)}, u32[]{:S(2)}) async-start(f32[8,32,256]{2,1,0:T(8,128)} %bitcast.2), calls=%async_computation.2 | async-start | bytes 524288 | tf_op jit(solution)/shard_map/all_to_all | solution.py:131
  65.6 47.1 %reduce-scatter.2.cloned.1.call-start = ((), (), s32[]{:S(2)}) async-start(), calls=%async_computation.3 | async-start | bytes 294912 | tf_op jit(solution)/shard_map/reduce_scatter | solution.py:137
  113.4 3.1 %collective-permute-start = (f32[16,256]{1,0:T(8,128)S(1)}, f32[16,256]{1,0:T(8,128)S(1)}, u32[]{:S(2)}, u32[]{:S(2)}) collective-permute-start(f32[16,256]{1,0:T(8,128)S(1)} %constant_dynamic-slice_fusion), channel_id=1, source_target_pairs={{0,1},{1,0},{2,3},{3,2},{4,5},{5,4},{6,7},{7,6},{8,9},{9,8},{10,11... | collective-permute-start | bytes 49160 | tf_op jit(solution)/shard_map/ppermute | solution.py:146
Sparse Core Ops, SparseCore 0:
  69.8 42.8 reduce-scatter.1

commit v3 on v2

--- a/solution.py
+++ b/solution.py
@@ -30,10 +30,10 @@
     return jnp.where(row == col, value, 0.0).astype(F32)
 
 
-def local_kernel(scales, sizes, x_hbm, y_hbm, c_hbm, pat_hbm, cnt_hbm, item_ref, user_ref,
+def local_kernel(scales, sizes, x_hbm, y_hbm, c_hbm, pat_hbm, cnt_hbm, item_ref, keep_ref, send_ref,
                  x_ref, y_ref, c_ref, pat, cnt, s_ref, w_ref, sems):
     item_scale, item_gram, item_ridge, user_scale, user_gram, user_ridge = scales
-    x_size, zh_size, zl_size = sizes
+    x_size, zh_size, zl_size, y_size, core_size = sizes
     user_tiles, _, slots, tile, _ = c_ref.shape
     width = x_ref.shape[1]
     item_rows = y_ref.shape[0]
@@ -65,7 +65,7 @@
     gx_high, gx_low = split(dot(x, x, ((0,), (0,))) * item_gram + eye(width, item_ridge))
     y = y_ref[...]
     gy_high, gy_low = split(dot(y, y, ((0,), (0,))) * user_gram + eye(width, user_ridge))
-    user = jnp.zeros(user_ref.shape, F32)
+    user = jnp.zeros(x_ref.shape, F32)
     for t in range(item_tiles):
         y_t = y_ref[t * tile:(t + 1) * tile, :]
         high, low = split(w_ref[t])
@@ -79,7 +79,31 @@
             place = ((xi * zl_size + zl) * zh_size + zh) * owner_rows + offset
             item_ref[place:place + block, :] = whole[k:k + block, :]
     gram = dot(x, gy_high, ((1,), (0,))) + dot(x, gy_low, ((1,), (0,)))
-    user_ref[...] = user * user_scale + gram
+    user = user * user_scale + gram
+    half = keep_ref.shape[0]
+    share = 2 * half // (y_size * core_size)
+    my_y, my_core = lax.axis_index("y"), lax.axis_index("core")
+    for k in range(y_size * core_size):
+        rows = user[k * share:(k + 1) * share, :]
+        place = jnp.int32(0)
+        bit = half
+        for dest, mine, size in ((k % core_size, my_core, core_size), (k // core_size, my_y, y_size)):
+            for level in range(size.bit_length() - 1):
+                differs = (mine // 2 ** level + dest // 2 ** level) % 2
+                if bit == half:
+                    away = differs
+                else:
+                    place += differs * bit
+                bit //= 2
+        place = pl.multiple_of(place, share)
+
+        @pl.when(away == 0)
+        def _():
+            keep_ref[pl.ds(place, share), :] = rows
+
+        @pl.when(away == 1)
+        def _():
+            send_ref[pl.ds(place, share), :] = rows
 
 
 def shards(user_factors, item_factors, pattern, counts, confidence):
@@ -99,16 +123,18 @@
         2.0 / norm_item, 2.0 * WEIGHT_ALL / users_total, 2.0 * RIDGE_COEF / user_size,
         2.0 / norm_user, 2.0 * WEIGHT_ALL / items_total, 2.0 * RIDGE_COEF / item_size,
     )
-    sizes = tuple(lax.axis_size(name) for name in USERS)
+    sizes = tuple(lax.axis_size(name) for name in USERS + ITEMS)
 
-    item_part, user_part = pl.pallas_call(
+    item_part, keep, send = pl.pallas_call(
         lambda *refs: local_kernel(scales, sizes, *refs),
         out_shape=(
             jax.ShapeDtypeStruct((item_rows, feat_width), F32),
-            jax.ShapeDtypeStruct((user_rows, feat_width), F32),
+            jax.ShapeDtypeStruct((user_rows // 2, feat_width), F32),
+            jax.ShapeDtypeStruct((user_rows // 2, feat_width), F32),
         ),
         in_specs=[pl.BlockSpec(memory_space=pltpu.HBM)] * 5,
         out_specs=(
+            pl.BlockSpec(memory_space=pltpu.VMEM),
             pl.BlockSpec(memory_space=pltpu.VMEM),
             pl.BlockSpec(memory_space=pltpu.VMEM),
         ),
@@ -126,24 +152,24 @@
         name="local_sums",
     )(user_factors, item_factors, confidence, pattern, counts.T)
 
-    def reduce_over(part, axes):
+    def exchange(part, axes):
         size = lax.axis_size(axes)
         moved = lax.all_to_all(part, axes, 0, 0, tiled=True)
-        return moved.reshape(size, part.shape[0] // size, feat_width).sum(0)
+        return moved.reshape(size, part.shape[0] // size, feat_width)
 
-    item_half = reduce_over(item_part, ("x", "zl"))
-    item_gradient = reduce_over(item_half, "zh")
+    def halve(keep, send, name, distance):
+        pairs = [(i, i ^ distance) for i in range(lax.axis_size(name))]
+        whole = keep + lax.ppermute(send, name, pairs)
+        half = whole.shape[0] // 2
+        return whole[:half], whole[half:], whole
 
-    user_pair = lax.psum_scatter(user_part, "y", scatter_dimension=0, tiled=True)
-    cores = lax.axis_size("core")
-    share_rows = user_pair.shape[0] // cores
-    core = lax.axis_index("core")
-    mine = lax.dynamic_slice_in_dim(user_pair, core * share_rows, share_rows, 0)
-    if cores == 1:
-        user_gradient = mine
-    else:
-        other = lax.dynamic_slice_in_dim(user_pair, (1 - core) * share_rows, share_rows, 0)
-        user_gradient = mine + lax.ppermute(other, "core", [(0, 1), (1, 0)])
+    steps = [(name, 2 ** level) for name in ("core", "y") for level in range(lax.axis_size(name).bit_length() - 1)]
+    moved = exchange(item_part, ("x", "zl"))
+    for step in steps[:-1]:
+        keep, send, _ = halve(keep, send, *step)
+    moved, keep, send = lax.optimization_barrier((moved, keep, send))
+    item_gradient = exchange(moved.sum(0), "zh").sum(0)
+    user_gradient = halve(keep, send, *steps[-1])[2]
     return (user_gradient, item_gradient[None])
 
 

time: 127 us -> 80.3 us (0.63); the launches traced: 125 us -> 79.9 us
  blocking collectives: 33.4 us -> 0 us
  starting transfers between devices: 19.8 us -> 38 us
  waiting for transfers between devices: 48.2 us -> 32.3 us
  between operations: 14.1 us -> 0.72 us
    reduce_scatter x1 -> x0, waiting for transfers between devices: 46.4 us -> none  [shards(): lax.psum_scatter(user_part, 'y', scatter_dimension=0, tiled=True)]
    all_to_all x1 -> x0, blocking collectives: 33.4 us -> none  [reduce_over(): moved = lax.all_to_all(part, axes, 0, 0, tiled=True)]
    all_to_all x1 -> x2, waiting for transfers between devices: 0.01 us -> 20.6 us  [exchange(): moved = lax.all_to_all(part, axes, 0, 0, tiled=True)]
    ppermute x1 -> x4, starting transfers between devices: 1.91 us -> 13.9 us  [halve(): whole = keep + lax.ppermute(send, name, pairs)]
    ppermute x1 -> x4, waiting for transfers between devices: 1.15 us -> 11.7 us  [halve(): whole = keep + lax.ppermute(send, name, pairs)]
    all_to_all x1 -> x2, starting transfers between devices: 17.9 us -> 24.1 us  [exchange(): moved = lax.all_to_all(part, axes, 0, 0, tiled=True)]
  transfers between devices with their start and end apart: 3 -> 6, of which waited for: 2 -> 6; matrix products, arithmetic and copies ran while one was open for 2% -> 1% of each run, Pallas kernels for 0% -> 0%
where the time goes in v3:
time: 80.3 us; the launch traced here: 79.9 us
  starting transfers between devices  38 us (47%)
  waiting for transfers between devices  32.3 us (40%)
  Pallas kernels  6.71 us (8%)
  other arithmetic  2.12 us (3%)
    all_to_all x2, starting transfers between devices, exchange(): moved = lax.all_to_all(part, axes, 0, 0, tiled=True)  24.1 us
    all_to_all x2, waiting for transfers between devices, exchange(): moved = lax.all_to_all(part, axes, 0, 0, tiled=True)  20.6 us
    ppermute x4, starting transfers between devices, halve(): whole = keep + lax.ppermute(send, name, pairs)  13.9 us
    ppermute x4, waiting for transfers between devices, halve(): whole = keep + lax.ppermute(send, name, pairs)  11.7 us
    pallas_call x1, Pallas kernels, shards(): pl.pallas_call(lambda *refs: local_kernel(scales, sizes, *refs), out_shap...  6.71 us
  transfers between devices with their start and end apart: 6, of which 6 were waited for; matrix products, arithmetic and copies ran while one was open for 1% of the time, Pallas kernels for 0%

profile of v3, /device:TPU:56, one launch (start us, length us, event | category | flops | bytes accessed | tf_op | source)
XLA Modules:
  0.0 79.9 jit_solution(8985184204005964532)
XLA Ops:
  0.6 6.7 %local_sums.1 = (f32[2048,256]{1,0:T(8,128)}, f32[128,256]{1,0:T(8,128)}, f32[128,256]{1,0:T(8,128)}) custom-call(bf16[256,256]{1,0:T(8,128)(2,1)} %refs_0_.1, bf16[2048,256]{1,0:T(8,128)(2,1)} %refs_1_.1, bf16[2,1,16,128,128]{4,3,2,1,0:T(8,128)(2,1)} %refs_2_.1, s32[2,1,16]{2,1,0:T(1,128)} %refs_3_.1, s32[1,2]{1,0:T(1,128)} %bitcast.6), custom_call_target="tpu_custom_call" | custom-call | tf_op jit(solution)/shard_map/local_sums/pallas_call | solution.py:128
  7.3 0.0 copy-start.1
  7.4 0.0 copy-start
  7.4 6.3 %all-to-all-start = ((f32[8,256,256]{2,1,0:T(8,128)}), f32[8,256,256]{2,1,0:T(8,128)S(1)}, u32[]{:S(2)}, u32[]{:S(2)}) async-start(f32[8,256,256]{2,1,0:T(8,128)} %bitcast.4), calls=%async_computation | async-start | bytes 4194304 | tf_op jit(solution)/shard_map/all_to_all | solution.py:157
  13.6 0.0 copy-done.1
  13.6 1.9 %collective-permute-start = (f32[128,256]{1,0:T(8,128)S(1)}, f32[128,256]{1,0:T(8,128)S(1)}, u32[]{:S(2)}, u32[]{:S(2)}) collective-permute-start(f32[128,256]{1,0:T(8,128)S(1)} %copy-done.1), channel_id=1, source_target_pairs={{0,1},{1,0},{2,3},{3,2},{4,5},{5,4},{6,7},{7,6},{8,9},{9,8},{10,11... | collective-permute-start | bytes 393224 | tf_op jit(solution)/shard_map/ppermute | solution.py:162
  15.6 1.3 %collective-permute-done = f32[128,256]{1,0:T(8,128)S(1)} collective-permute-done((f32[128,256]{1,0:T(8,128)S(1)}, f32[128,256]{1,0:T(8,128)S(1)}, u32[]{:S(2)}, u32[]{:S(2)}) %collective-permute-start) | collective-permute-done | bytes 131104 | tf_op jit(solution)/shard_map/ppermute | solution.py:162
  16.9 0.0 copy-done
  16.9 3.3 %collective-permute-start.1 = (f32[64,256]{1,0:T(8,128)S(1)}, f32[64,256]{1,0:T(8,128)S(1)}, u32[]{:S(2)}, u32[]{:S(2)}) collective-permute-start(f32[64,256]{1,0:T(8,128)S(1)} %slice.25), channel_id=1, source_target_pairs={{0,2},{2,0},{4,6},{6,4},{8,10},{10,8},{12,14},{14,12},{1,3},{3,1},... | collective-permute-start | bytes 196616 | tf_op jit(solution)/shard_map/ppermute | solution.py:162
  20.2 2.9 %collective-permute-done.1 = f32[64,256]{1,0:T(8,128)S(1)} collective-permute-done((f32[64,256]{1,0:T(8,128)S(1)}, f32[64,256]{1,0:T(8,128)S(1)}, u32[]{:S(2)}, u32[]{:S(2)}) %collective-permute-start.1) | collective-permute-done | bytes 65568 | tf_op jit(solution)/shard_map/ppermute | solution.py:162
  23.1 4.0 %collective-permute-start.2 = (f32[32,256]{1,0:T(8,128)S(1)}, f32[32,256]{1,0:T(8,128)S(1)}, u32[]{:S(2)}, u32[]{:S(2)}) collective-permute-start(f32[32,256]{1,0:T(8,128)S(1)} %slice.27), channel_id=1, source_target_pairs={{0,4},{2,6},{4,0},{6,2},{8,12},{10,14},{12,8},{14,10},{1,5},{3,7},... | collective-permute-start | bytes 98312 | tf_op jit(solution)/shard_map/ppermute | solution.py:162
  27.1 2.7 %collective-permute-done.2 = f32[32,256]{1,0:T(8,128)S(1)} collective-permute-done((f32[32,256]{1,0:T(8,128)S(1)}, f32[32,256]{1,0:T(8,128)S(1)}, u32[]{:S(2)}, u32[]{:S(2)}) %collective-permute-start.2) | collective-permute-done | bytes 32800 | tf_op jit(solution)/shard_map/ppermute | solution.py:162
  29.8 10.8 %all-to-all-done = f32[8,256,256]{2,1,0:T(8,128)S(1)} async-done(((f32[8,256,256]{2,1,0:T(8,128)}), f32[8,256,256]{2,1,0:T(8,128)S(1)}, u32[]{:S(2)}, u32[]{:S(2)}) %all-to-all-start) | async-done | bytes 2097184 | tf_op jit(solution)/shard_map/all_to_all | solution.py:157
  40.6 0.8 %reduce_sum.18 = f32[256,256]{1,0:T(8,128)} reduce(f32[8,256,256]{2,1,0:T(8,128)S(1)} %all-to-all-done, f32[]{:T(128)} %constant.0.clone.1), dimensions={0}, to_apply=%region_0.0 | reduce | flops 458752 | bytes 2359300 | tf_op jit(solution)/shard_map/reduce_sum | solution.py:171
  41.4 17.8 %all-to-all-start.1 = ((f32[8,32,256]{2,1,0:T(8,128)}), f32[8,32,256]{2,1,0:T(8,128)S(1)}, u32[]{:S(2)}, u32[]{:S(2)}) async-start(f32[8,32,256]{2,1,0:T(8,128)} %bitcast.2), calls=%async_computation.1 | async-start | bytes 524288 | tf_op jit(solution)/shard_map/all_to_all | solution.py:157
  59.3 4.7 %collective-permute-start.3 = (f32[16,256]{1,0:T(8,128)S(1)}, f32[16,256]{1,0:T(8,128)S(1)}, u32[]{:S(2)}, u32[]{:S(2)}) collective-permute-start(f32[16,256]{1,0:T(8,128)S(1)} %get-tuple-element.12), channel_id=1, source_target_pairs={{0,8},{2,10},{4,12},{6,14},{8,0},{10,2},{12,4},{14,6},{1,9},{3,11}... | collective-permute-start | bytes 49160 | tf_op jit(solution)/shard_map/ppermute | solution.py:162
  64.0 4.8 %collective-permute-done.3 = f32[16,256]{1,0:T(8,128)S(1)} collective-permute-done((f32[16,256]{1,0:T(8,128)S(1)}, f32[16,256]{1,0:T(8,128)S(1)}, u32[]{:S(2)}, u32[]{:S(2)}) %collective-permute-start.3) | collective-permute-done | bytes 16416 | tf_op jit(solution)/shard_map/ppermute | solution.py:162
  68.8 0.6 add.15
  69.4 9.8 %all-to-all-done.1 = f32[8,32,256]{2,1,0:T(8,128)S(1)} async-done(((f32[8,32,256]{2,1,0:T(8,128)}), f32[8,32,256]{2,1,0:T(8,128)S(1)}, u32[]{:S(2)}, u32[]{:S(2)}) %all-to-all-start.1) | async-done | bytes 262176 | tf_op jit(solution)/shard_map/all_to_all | solution.py:157
  79.2 0.6 reduce_sum.19
  (6 shorter events, 0.1 us)
Async XLA Ops:
  7.3 6.3 %copy-start.1 = (f32[128,256]{1,0:T(8,128)S(1)}, f32[128,256]{1,0:T(8,128)}, u32[]{:S(2)}) copy-start(f32[128,256]{1,0:T(8,128)} %get-tuple-element.10) | copy-start | bytes 393220
  7.4 9.5 %copy-start = (f32[128,256]{1,0:T(8,128)S(1)}, f32[128,256]{1,0:T(8,128)}, u32[]{:S(2)}) copy-start(f32[128,256]{1,0:T(8,128)} %get-tuple-element.9) | copy-start | bytes 393220
  7.4 33.2 %all-to-all-start = ((f32[8,256,256]{2,1,0:T(8,128)}), f32[8,256,256]{2,1,0:T(8,128)S(1)}, u32[]{:S(2)}, u32[]{:S(2)}) async-start(f32[8,256,256]{2,1,0:T(8,128)} %bitcast.4), calls=%async_computation | async-start | bytes 4194304 | tf_op jit(solution)/shard_map/all_to_all | solution.py:157
  13.6 3.2 %collective-permute-start = (f32[128,256]{1,0:T(8,128)S(1)}, f32[128,256]{1,0:T(8,128)S(1)}, u32[]{:S(2)}, u32[]{:S(2)}) collective-permute-start(f32[128,256]{1,0:T(8,128)S(1)} %copy-done.1), channel_id=1, source_target_pairs={{0,1},{1,0},{2,3},{3,2},{4,5},{5,4},{6,7},{7,6},{8,9},{9,8},{10,11... | collective-permute-start | bytes 393224 | tf_op jit(solution)/shard_map/ppermute | solution.py:162
  16.9 6.2 %collective-permute-start.1 = (f32[64,256]{1,0:T(8,128)S(1)}, f32[64,256]{1,0:T(8,128)S(1)}, u32[]{:S(2)}, u32[]{:S(2)}) collective-permute-start(f32[64,256]{1,0:T(8,128)S(1)} %slice.25), channel_id=1, source_target_pairs={{0,2},{2,0},{4,6},{6,4},{8,10},{10,8},{12,14},{14,12},{1,3},{3,1},... | collective-permute-start | bytes 196616 | tf_op jit(solution)/shard_map/ppermute | solution.py:162
  23.1 6.7 %collective-permute-start.2 = (f32[32,256]{1,0:T(8,128)S(1)}, f32[32,256]{1,0:T(8,128)S(1)}, u32[]{:S(2)}, u32[]{:S(2)}) collective-permute-start(f32[32,256]{1,0:T(8,128)S(1)} %slice.27), channel_id=1, source_target_pairs={{0,4},{2,6},{4,0},{6,2},{8,12},{10,14},{12,8},{14,10},{1,5},{3,7},... | collective-permute-start | bytes 98312 | tf_op jit(solution)/shard_map/ppermute | solution.py:162
  41.4 37.8 %all-to-all-start.1 = ((f32[8,32,256]{2,1,0:T(8,128)}), f32[8,32,256]{2,1,0:T(8,128)S(1)}, u32[]{:S(2)}, u32[]{:S(2)}) async-start(f32[8,32,256]{2,1,0:T(8,128)} %bitcast.2), calls=%async_computation.1 | async-start | bytes 524288 | tf_op jit(solution)/shard_map/all_to_all | solution.py:157
  59.3 9.5 %collective-permute-start.3 = (f32[16,256]{1,0:T(8,128)S(1)}, f32[16,256]{1,0:T(8,128)S(1)}, u32[]{:S(2)}, u32[]{:S(2)}) collective-permute-start(f32[16,256]{1,0:T(8,128)S(1)} %get-tuple-element.12), channel_id=1, source_target_pairs={{0,8},{2,10},{4,12},{6,14},{8,0},{10,2},{12,4},{14,6},{1,9},{3,11}... | collective-permute-start | bytes 49160 | tf_op jit(solution)/shard_map/ppermute | solution.py:162

commit v4 on v3

--- a/solution.py
+++ b/solution.py
@@ -30,46 +30,54 @@
     return jnp.where(row == col, value, 0.0).astype(F32)
 
 
-def local_kernel(scales, sizes, x_hbm, y_hbm, c_hbm, pat_hbm, cnt_hbm, item_ref, keep_ref, send_ref,
-                 x_ref, y_ref, c_ref, pat, cnt, s_ref, w_ref, sems):
-    item_scale, item_gram, item_ridge, user_scale, user_gram, user_ridge = scales
-    x_size, zh_size, zl_size, y_size, core_size = sizes
+def item_kernel(scales, sizes, x_hbm, y_hbm, c_hbm, pat_hbm, cnt_hbm, item_hbm, high_hbm, low_hbm,
+                x_ref, y_ref, c_ref, pat, cnt, s_ref, w_ref, high_ref, low_ref, item_ref, in_sems, out_sems):
+    item_scale, item_gram, item_ridge = scales
+    x_size, zh_size, zl_size = sizes
     user_tiles, _, slots, tile, _ = c_ref.shape
     width = x_ref.shape[1]
     item_rows = y_ref.shape[0]
     item_tiles = item_rows // tile
     owner_rows = item_rows // (x_size * zh_size * zl_size)
     block = min(tile, owner_rows)
-    copies = [
-        pltpu.make_async_copy(src, dst, sems.at[k])
-        for k, (src, dst) in enumerate(
-            ((x_hbm, x_ref), (y_hbm, y_ref), (pat_hbm, pat), (cnt_hbm, cnt), (c_hbm, c_ref)))
-    ]
-    for copy in copies:
-        copy.start()
+    parts = 4
+    span = item_rows // parts
+    moves = [(x_hbm, x_ref), (pat_hbm, pat), (cnt_hbm, cnt)]
+    moves += [(y_hbm.at[pl.ds(k * span, span)], y_ref.at[pl.ds(k * span, span)]) for k in range(parts)]
+    moves += [(c_hbm.at[b], c_ref.at[b]) for b in range(user_tiles)]
+    loads = [pltpu.make_async_copy(src, dst, in_sems.at[k]) for k, (src, dst) in enumerate(moves)]
+    for load in loads:
+        load.start()
     w_ref[...] = jnp.zeros_like(w_ref)
-    copies[0].wait()
-    copies[1].wait()
+    loads[0].wait()
     x = x_ref[...]
+    gx_high, gx_low = split(dot(x, x, ((0,), (0,))) * item_gram + eye(width, item_ridge))
     for t in range(item_tiles):
+        if t * tile % span == 0:
+            loads[3 + t * tile // span].wait()
         s_ref[t] = dot(x, y_ref[t * tile:(t + 1) * tile, :], ((1,), (1,))) - 1.0
-    for copy in copies[2:]:
-        copy.wait()
+    loads[1].wait()
+    loads[2].wait()
     for b in range(user_tiles):
+        loads[3 + parts + b].wait()
         rows = pl.ds(b * tile, tile)
         for s in range(slots):
             t = pat[b, 0, s]
             live = jnp.where(s < cnt[0, b], 1.0, 0.0).astype(F32)
             residual = (live * c_ref[b, 0, s].astype(F32) * s_ref[t, rows, :]).astype(BF16)
             w_ref[t, rows, :] += residual.astype(F32)
-    gx_high, gx_low = split(dot(x, x, ((0,), (0,))) * item_gram + eye(width, item_ridge))
-    y = y_ref[...]
-    gy_high, gy_low = split(dot(y, y, ((0,), (0,))) * user_gram + eye(width, user_ridge))
-    user = jnp.zeros(x_ref.shape, F32)
+    stores = []
+
+    def store(src, dst):
+        copy = pltpu.make_async_copy(src, dst, out_sems.at[len(stores)])
+        copy.start()
+        stores.append(copy)
+
     for t in range(item_tiles):
         y_t = y_ref[t * tile:(t + 1) * tile, :]
         high, low = split(w_ref[t])
-        user += dot(high, y_t, ((1,), (0,))) + dot(low, y_t, ((1,), (0,)))
+        high_ref[t] = high
+        low_ref[t] = low
         part = dot(high, x, ((0,), (0,))) + dot(low, x, ((0,), (0,)))
         gram = dot(y_t, gx_high, ((1,), (0,))) + dot(y_t, gx_low, ((1,), (0,)))
         whole = part * item_scale + gram
@@ -78,6 +86,41 @@
             xi, zh, zl = owner // (zh_size * zl_size), owner // zl_size % zh_size, owner % zl_size
             place = ((xi * zl_size + zl) * zh_size + zh) * owner_rows + offset
             item_ref[place:place + block, :] = whole[k:k + block, :]
+        if owner_rows < tile:
+            count = tile // (owner_rows * zl_size)
+            zh = t * tile // (owner_rows * zl_size) % zh_size
+            for zl in range(zl_size):
+                first = ((xi * zl_size + zl) * zh_size + zh) * owner_rows
+                where = pl.ds(first, count * owner_rows)
+                store(item_ref.at[where], item_hbm.at[where])
+    if owner_rows >= tile:
+        store(item_ref, item_hbm)
+    store(high_ref, high_hbm)
+    store(low_ref, low_hbm)
+    for copy in stores:
+        copy.wait()
+
+
+def user_kernel(scales, sizes, x_hbm, y_hbm, high_hbm, low_hbm, keep_ref, send_ref,
+                x_ref, y_ref, high_ref, low_ref, in_sems):
+    user_scale, user_gram, user_ridge = scales
+    y_size, core_size = sizes
+    item_tiles, _, tile = high_ref.shape
+    width = x_ref.shape[1]
+    moves = ((y_hbm, y_ref), (x_hbm, x_ref), (high_hbm, high_ref), (low_hbm, low_ref))
+    loads = [pltpu.make_async_copy(src, dst, in_sems.at[k]) for k, (src, dst) in enumerate(moves)]
+    for load in loads:
+        load.start()
+    loads[0].wait()
+    y = y_ref[...]
+    gy_high, gy_low = split(dot(y, y, ((0,), (0,))) * user_gram + eye(width, user_ridge))
+    for load in loads[1:]:
+        load.wait()
+    x = x_ref[...]
+    user = jnp.zeros(x_ref.shape, F32)
+    for t in range(item_tiles):
+        y_t = y_ref[t * tile:(t + 1) * tile, :]
+        user += dot(high_ref[t], y_t, ((1,), (0,))) + dot(low_ref[t], y_t, ((1,), (0,)))
     gram = dot(x, gy_high, ((1,), (0,))) + dot(x, gy_low, ((1,), (0,)))
     user = user * user_scale + gram
     half = keep_ref.shape[0]
@@ -119,38 +162,60 @@
     items_total = item_rows * item_size
     norm_user = math.sqrt(slot_count * item_size * tile_rows)
     norm_item = math.sqrt(users_total * slot_count / item_tiles)
-    scales = (
-        2.0 / norm_item, 2.0 * WEIGHT_ALL / users_total, 2.0 * RIDGE_COEF / user_size,
-        2.0 / norm_user, 2.0 * WEIGHT_ALL / items_total, 2.0 * RIDGE_COEF / item_size,
-    )
-    sizes = tuple(lax.axis_size(name) for name in USERS + ITEMS)
-
-    item_part, keep, send = pl.pallas_call(
-        lambda *refs: local_kernel(scales, sizes, *refs),
+    item_scales = (2.0 / norm_item, 2.0 * WEIGHT_ALL / users_total, 2.0 * RIDGE_COEF / user_size)
+    user_scales = (2.0 / norm_user, 2.0 * WEIGHT_ALL / items_total, 2.0 * RIDGE_COEF / item_size)
+    user_axes = tuple(lax.axis_size(name) for name in USERS)
+    item_axes = tuple(lax.axis_size(name) for name in ITEMS)
+    in_hbm = pl.BlockSpec(memory_space=pltpu.HBM)
+    in_vmem = pl.BlockSpec(memory_space=pltpu.VMEM)
+    params = pltpu.CompilerParams(vmem_limit_bytes=32 * 1024 * 1024)
+    sums_shape = (item_tiles, user_rows, tile_rows)
+
+    def pinned(*arrays):
+        return [pltpu.with_memory_space_constraint(a, pltpu.HBM) for a in arrays]
+
+    item_part, high, low = pl.pallas_call(
+        lambda *refs: item_kernel(item_scales, user_axes, *refs),
         out_shape=(
-            jax.ShapeDtypeStruct((item_rows, feat_width), F32),
-            jax.ShapeDtypeStruct((user_rows // 2, feat_width), F32),
-            jax.ShapeDtypeStruct((user_rows // 2, feat_width), F32),
+            pltpu.HBM((item_rows, feat_width), F32),
+            pltpu.HBM(sums_shape, BF16),
+            pltpu.HBM(sums_shape, BF16),
         ),
-        in_specs=[pl.BlockSpec(memory_space=pltpu.HBM)] * 5,
-        out_specs=(
-            pl.BlockSpec(memory_space=pltpu.VMEM),
-            pl.BlockSpec(memory_space=pltpu.VMEM),
-            pl.BlockSpec(memory_space=pltpu.VMEM),
-        ),
+        in_specs=[in_hbm] * 5,
+        out_specs=(in_hbm,) * 3,
         scratch_shapes=[
             pltpu.VMEM(user_factors.shape, BF16),
             pltpu.VMEM(item_factors.shape, BF16),
             pltpu.VMEM(confidence.shape, BF16),
             pltpu.SMEM(pattern.shape, jnp.int32),
             pltpu.SMEM((1, user_tiles), jnp.int32),
-            pltpu.VMEM((item_tiles, user_rows, tile_rows), F32),
-            pltpu.VMEM((item_tiles, user_rows, tile_rows), F32),
-            pltpu.SemaphoreType.DMA((5,)),
+            pltpu.VMEM(sums_shape, F32),
+            pltpu.VMEM(sums_shape, F32),
+            pltpu.VMEM(sums_shape, BF16),
+            pltpu.VMEM(sums_shape, BF16),
+            pltpu.VMEM((item_rows, feat_width), F32),
+            pltpu.SemaphoreType.DMA((7 + user_tiles,)),
+            pltpu.SemaphoreType.DMA((2 + 2 * item_tiles,)),
         ],
-        compiler_params=pltpu.CompilerParams(vmem_limit_bytes=60 * 1024 * 1024),
-        name="local_sums",
-    )(user_factors, item_factors, confidence, pattern, counts.T)
+        compiler_params=params,
+        name="item_sums",
+    )(*pinned(user_factors, item_factors, confidence, pattern, counts.T))
+
+    keep, send = pl.pallas_call(
+        lambda *refs: user_kernel(user_scales, item_axes, *refs),
+        out_shape=(pltpu.VMEM((user_rows // 2, feat_width), F32),) * 2,
+        in_specs=[in_hbm] * 4,
+        out_specs=(in_vmem,) * 2,
+        scratch_shapes=[
+            pltpu.VMEM(user_factors.shape, BF16),
+            pltpu.VMEM(item_factors.shape, BF16),
+            pltpu.VMEM(sums_shape, BF16),
+            pltpu.VMEM(sums_shape, BF16),
+            pltpu.SemaphoreType.DMA((4,)),
+        ],
+        compiler_params=params,
+        name="user_sums",
+    )(*pinned(user_factors, item_factors, high, low))
 
     def exchange(part, axes):
         size = lax.axis_size(axes)

time: 80.3 us -> 79.2 us (0.986)
  waiting for transfers between devices: 32.3 us -> 28.6 us
  Pallas kernels: 6.71 us -> 9.46 us
    all_to_all x2, waiting for transfers between devices: 20.6 us -> 16.9 us  [exchange(): moved = lax.all_to_all(part, axes, 0, 0, tiled=True)]
    pallas_call x1 -> x2, Pallas kernels: 6.71 us -> 9.46 us  [the longest x1 5.75 us: shards(): pl.pallas_call(lambda *refs: item_kernel(item_scales, user_axes, *refs),...]
  transfers between devices with their start and end apart: 6 -> 6, of which waited for: 6 -> 6; matrix products, arithmetic and copies ran while one was open for 1% -> 1% of each run, Pallas kernels for 0% -> 5%
where the time goes in v4:
time: 79.2 us; the launch traced here: 78.8 us
  starting transfers between devices  37.9 us (48%)
  waiting for transfers between devices  28.6 us (36%)
  Pallas kernels  9.46 us (12%)
  other arithmetic  2.12 us (3%)
    all_to_all x2, starting transfers between devices, exchange(): moved = lax.all_to_all(part, axes, 0, 0, tiled=True)  24 us
    all_to_all x2, waiting for transfers between devices, exchange(): moved = lax.all_to_all(part, axes, 0, 0, tiled=True)  16.9 us
    ppermute x4, starting transfers between devices, halve(): whole = keep + lax.ppermute(send, name, pairs)  13.9 us
    ppermute x4, waiting for transfers between devices, halve(): whole = keep + lax.ppermute(send, name, pairs)  11.7 us
    pallas_call x1, Pallas kernels, shards(): pl.pallas_call(lambda *refs: item_kernel(item_scales, user_axes, *refs),...  5.75 us
    pallas_call x1, Pallas kernels, shards(): pl.pallas_call(lambda *refs: user_kernel(user_scales, item_axes, *refs),...  3.71 us
  transfers between devices with their start and end apart: 6, of which 6 were waited for; matrix products, arithmetic and copies ran while one was open for 1% of the time, Pallas kernels for 5%

profile of v4, /device:TPU:56, one launch (start us, length us, event | category | flops | bytes accessed | tf_op | source)
XLA Modules:
  0.0 78.8 jit_solution(13959915594321085267)
XLA Ops:
  0.6 5.8 %item_sums.1 = (f32[2048,256]{1,0:T(8,128)}, bf16[16,256,128]{2,1,0:T(8,128)(2,1)}, bf16[16,256,128]{2,1,0:T(8,128)(2,1)}) custom-call(bf16[256,256]{1,0:T(8,128)(2,1)} %refs_0_.3, bf16[2048,256]{1,0:T(8,128)(2,1)} %refs_1_.3, bf16[2,1,16,128,128]{4,3,2,1,0:T(8,128)(2,1)} %refs_2_.1, s32[2,1,16]{2,1,0:T(1,128)} %refs_3_.1, s32[1,2]{1,0:T(1,128)} %bitcast.6), custom_call_target="tpu_custom_call" | custom-call | tf_op jit(solution)/shard_map/item_sums/pallas_call | solution.py:177
  6.4 6.1 %all-to-all-start = ((f32[8,256,256]{2,1,0:T(8,128)}), f32[8,256,256]{2,1,0:T(8,128)S(1)}, u32[]{:S(2)}, u32[]{:S(2)}) async-start(f32[8,256,256]{2,1,0:T(8,128)} %bitcast.4), calls=%async_computation | async-start | bytes 4194304 | tf_op jit(solution)/shard_map/all_to_all | solution.py:222
  12.5 3.7 %user_sums.1 = (f32[128,256]{1,0:T(8,128)S(1)}, f32[128,256]{1,0:T(8,128)S(1)}) custom-call(bf16[256,256]{1,0:T(8,128)(2,1)} %refs_0_.3, bf16[2048,256]{1,0:T(8,128)(2,1)} %refs_1_.3, bf16[16,256,128]{2,1,0:T(8,128)(2,1)} %get-tuple-element.11.refs_2_, bf16[16,256,128]{2,1,0:T(8,128)(2,1)} %get-tuple-element.12.refs_3_), custom_call_target="tpu_custom_call" | custom-call | tf_op jit(solution)/shard_map/user_sums/pallas_call | solution.py:204
  16.2 1.9 %collective-permute-start = (f32[128,256]{1,0:T(8,128)S(1)}, f32[128,256]{1,0:T(8,128)S(1)}, u32[]{:S(2)}, u32[]{:S(2)}) collective-permute-start(f32[128,256]{1,0:T(8,128)S(1)} %get-tuple-element.14), channel_id=1, source_target_pairs={{0,1},{1,0},{2,3},{3,2},{4,5},{5,4},{6,7},{7,6},{8,9},{9,8},{10,11... | collective-permute-start | bytes 393224 | tf_op jit(solution)/shard_map/ppermute | solution.py:227
  18.2 1.3 %collective-permute-done = f32[128,256]{1,0:T(8,128)S(1)} collective-permute-done((f32[128,256]{1,0:T(8,128)S(1)}, f32[128,256]{1,0:T(8,128)S(1)}, u32[]{:S(2)}, u32[]{:S(2)}) %collective-permute-start) | collective-permute-done | bytes 131104 | tf_op jit(solution)/shard_map/ppermute | solution.py:227
  19.5 3.3 %collective-permute-start.1 = (f32[64,256]{1,0:T(8,128)S(1)}, f32[64,256]{1,0:T(8,128)S(1)}, u32[]{:S(2)}, u32[]{:S(2)}) collective-permute-start(f32[64,256]{1,0:T(8,128)S(1)} %slice.25), channel_id=1, source_target_pairs={{0,2},{2,0},{4,6},{6,4},{8,10},{10,8},{12,14},{14,12},{1,3},{3,1},... | collective-permute-start | bytes 196616 | tf_op jit(solution)/shard_map/ppermute | solution.py:227
  22.8 2.9 %collective-permute-done.1 = f32[64,256]{1,0:T(8,128)S(1)} collective-permute-done((f32[64,256]{1,0:T(8,128)S(1)}, f32[64,256]{1,0:T(8,128)S(1)}, u32[]{:S(2)}, u32[]{:S(2)}) %collective-permute-start.1) | collective-permute-done | bytes 65568 | tf_op jit(solution)/shard_map/ppermute | solution.py:227
  25.7 4.0 %collective-permute-start.2 = (f32[32,256]{1,0:T(8,128)S(1)}, f32[32,256]{1,0:T(8,128)S(1)}, u32[]{:S(2)}, u32[]{:S(2)}) collective-permute-start(f32[32,256]{1,0:T(8,128)S(1)} %slice.27), channel_id=1, source_target_pairs={{0,4},{2,6},{4,0},{6,2},{8,12},{10,14},{12,8},{14,10},{1,5},{3,7},... | collective-permute-start | bytes 98312 | tf_op jit(solution)/shard_map/ppermute | solution.py:227
  29.7 2.7 %collective-permute-done.2 = f32[32,256]{1,0:T(8,128)S(1)} collective-permute-done((f32[32,256]{1,0:T(8,128)S(1)}, f32[32,256]{1,0:T(8,128)S(1)}, u32[]{:S(2)}, u32[]{:S(2)}) %collective-permute-start.2) | collective-permute-done | bytes 32800 | tf_op jit(solution)/shard_map/ppermute | solution.py:227
  32.4 7.1 %all-to-all-done = f32[8,256,256]{2,1,0:T(8,128)S(1)} async-done(((f32[8,256,256]{2,1,0:T(8,128)}), f32[8,256,256]{2,1,0:T(8,128)S(1)}, u32[]{:S(2)}, u32[]{:S(2)}) %all-to-all-start) | async-done | bytes 2097184 | tf_op jit(solution)/shard_map/all_to_all | solution.py:222
  39.5 0.8 %reduce_sum.18 = f32[256,256]{1,0:T(8,128)} reduce(f32[8,256,256]{2,1,0:T(8,128)S(1)} %all-to-all-done, f32[]{:T(128)} %constant.0.clone.1), dimensions={0}, to_apply=%region_0.0 | reduce | flops 458752 | bytes 2359300 | tf_op jit(solution)/shard_map/reduce_sum | solution.py:236
  40.3 17.8 %all-to-all-start.1 = ((f32[8,32,256]{2,1,0:T(8,128)}), f32[8,32,256]{2,1,0:T(8,128)S(1)}, u32[]{:S(2)}, u32[]{:S(2)}) async-start(f32[8,32,256]{2,1,0:T(8,128)} %bitcast.2), calls=%async_computation.1 | async-start | bytes 524288 | tf_op jit(solution)/shard_map/all_to_all | solution.py:222
  58.2 4.7 %collective-permute-start.3 = (f32[16,256]{1,0:T(8,128)S(1)}, f32[16,256]{1,0:T(8,128)S(1)}, u32[]{:S(2)}, u32[]{:S(2)}) collective-permute-start(f32[16,256]{1,0:T(8,128)S(1)} %get-tuple-element.16), channel_id=1, source_target_pairs={{0,8},{2,10},{4,12},{6,14},{8,0},{10,2},{12,4},{14,6},{1,9},{3,11}... | collective-permute-start | bytes 49160 | tf_op jit(solution)/shard_map/ppermute | solution.py:227
  62.9 4.8 %collective-permute-done.3 = f32[16,256]{1,0:T(8,128)S(1)} collective-permute-done((f32[16,256]{1,0:T(8,128)S(1)}, f32[16,256]{1,0:T(8,128)S(1)}, u32[]{:S(2)}, u32[]{:S(2)}) %collective-permute-start.3) | collective-permute-done | bytes 16416 | tf_op jit(solution)/shard_map/ppermute | solution.py:227
  67.7 0.6 add.15
  68.3 9.9 %all-to-all-done.1 = f32[8,32,256]{2,1,0:T(8,128)S(1)} async-done(((f32[8,32,256]{2,1,0:T(8,128)}), f32[8,32,256]{2,1,0:T(8,128)S(1)}, u32[]{:S(2)}, u32[]{:S(2)}) %all-to-all-start.1) | async-done | bytes 262176 | tf_op jit(solution)/shard_map/all_to_all | solution.py:222
  78.2 0.6 reduce_sum.19
  (6 shorter events, 0.1 us)
Async XLA Ops:
  6.4 33.1 %all-to-all-start = ((f32[8,256,256]{2,1,0:T(8,128)}), f32[8,256,256]{2,1,0:T(8,128)S(1)}, u32[]{:S(2)}, u32[]{:S(2)}) async-start(f32[8,256,256]{2,1,0:T(8,128)} %bitcast.4), calls=%async_computation | async-start | bytes 4194304 | tf_op jit(solution)/shard_map/all_to_all | solution.py:222
  16.2 3.2 %collective-permute-start = (f32[128,256]{1,0:T(8,128)S(1)}, f32[128,256]{1,0:T(8,128)S(1)}, u32[]{:S(2)}, u32[]{:S(2)}) collective-permute-start(f32[128,256]{1,0:T(8,128)S(1)} %get-tuple-element.14), channel_id=1, source_target_pairs={{0,1},{1,0},{2,3},{3,2},{4,5},{5,4},{6,7},{7,6},{8,9},{9,8},{10,11... | collective-permute-start | bytes 393224 | tf_op jit(solution)/shard_map/ppermute | solution.py:227
  19.5 6.2 %collective-permute-start.1 = (f32[64,256]{1,0:T(8,128)S(1)}, f32[64,256]{1,0:T(8,128)S(1)}, u32[]{:S(2)}, u32[]{:S(2)}) collective-permute-start(f32[64,256]{1,0:T(8,128)S(1)} %slice.25), channel_id=1, source_target_pairs={{0,2},{2,0},{4,6},{6,4},{8,10},{10,8},{12,14},{14,12},{1,3},{3,1},... | collective-permute-start | bytes 196616 | tf_op jit(solution)/shard_map/ppermute | solution.py:227
  25.7 6.7 %collective-permute-start.2 = (f32[32,256]{1,0:T(8,128)S(1)}, f32[32,256]{1,0:T(8,128)S(1)}, u32[]{:S(2)}, u32[]{:S(2)}) collective-permute-start(f32[32,256]{1,0:T(8,128)S(1)} %slice.27), channel_id=1, source_target_pairs={{0,4},{2,6},{4,0},{6,2},{8,12},{10,14},{12,8},{14,10},{1,5},{3,7},... | collective-permute-start | bytes 98312 | tf_op jit(solution)/shard_map/ppermute | solution.py:227
  40.3 37.8 %all-to-all-start.1 = ((f32[8,32,256]{2,1,0:T(8,128)}), f32[8,32,256]{2,1,0:T(8,128)S(1)}, u32[]{:S(2)}, u32[]{:S(2)}) async-start(f32[8,32,256]{2,1,0:T(8,128)} %bitcast.2), calls=%async_computation.1 | async-start | bytes 524288 | tf_op jit(solution)/shard_map/all_to_all | solution.py:222
  58.2 9.5 %collective-permute-start.3 = (f32[16,256]{1,0:T(8,128)S(1)}, f32[16,256]{1,0:T(8,128)S(1)}, u32[]{:S(2)}, u32[]{:S(2)}) collective-permute-start(f32[16,256]{1,0:T(8,128)S(1)} %get-tuple-element.16), channel_id=1, source_target_pairs={{0,8},{2,10},{4,12},{6,14},{8,0},{10,2},{12,4},{14,6},{1,9},{3,11}... | collective-permute-start | bytes 49160 | tf_op jit(solution)/shard_map/ppermute | solution.py:227

commit v5 on v4

--- a/solution.py
+++ b/solution.py
@@ -30,8 +30,8 @@
     return jnp.where(row == col, value, 0.0).astype(F32)
 
 
-def item_kernel(scales, sizes, x_hbm, y_hbm, c_hbm, pat_hbm, cnt_hbm, item_hbm, high_hbm, low_hbm,
-                x_ref, y_ref, c_ref, pat, cnt, s_ref, w_ref, high_ref, low_ref, item_ref, in_sems, out_sems):
+def item_kernel(scales, sizes, x_hbm, y_hbm, c_hbm, pat_hbm, cnt_hbm, item_hbm, high_ref, low_ref,
+                x_ref, y_ref, c_ref, pat, cnt, s_ref, w_ref, item_ref, in_sems, out_sems):
     item_scale, item_gram, item_ridge = scales
     x_size, zh_size, zl_size = sizes
     user_tiles, _, slots, tile, _ = c_ref.shape
@@ -40,10 +40,7 @@
     item_tiles = item_rows // tile
     owner_rows = item_rows // (x_size * zh_size * zl_size)
     block = min(tile, owner_rows)
-    parts = 4
-    span = item_rows // parts
-    moves = [(x_hbm, x_ref), (pat_hbm, pat), (cnt_hbm, cnt)]
-    moves += [(y_hbm.at[pl.ds(k * span, span)], y_ref.at[pl.ds(k * span, span)]) for k in range(parts)]
+    moves = [(x_hbm, x_ref), (pat_hbm, pat), (cnt_hbm, cnt), (y_hbm, y_ref)]
     moves += [(c_hbm.at[b], c_ref.at[b]) for b in range(user_tiles)]
     loads = [pltpu.make_async_copy(src, dst, in_sems.at[k]) for k, (src, dst) in enumerate(moves)]
     for load in loads:
@@ -52,14 +49,13 @@
     loads[0].wait()
     x = x_ref[...]
     gx_high, gx_low = split(dot(x, x, ((0,), (0,))) * item_gram + eye(width, item_ridge))
+    loads[3].wait()
     for t in range(item_tiles):
-        if t * tile % span == 0:
-            loads[3 + t * tile // span].wait()
         s_ref[t] = dot(x, y_ref[t * tile:(t + 1) * tile, :], ((1,), (1,))) - 1.0
     loads[1].wait()
     loads[2].wait()
     for b in range(user_tiles):
-        loads[3 + parts + b].wait()
+        loads[4 + b].wait()
         rows = pl.ds(b * tile, tile)
         for s in range(slots):
             t = pat[b, 0, s]
@@ -95,19 +91,17 @@
                 store(item_ref.at[where], item_hbm.at[where])
     if owner_rows >= tile:
         store(item_ref, item_hbm)
-    store(high_ref, high_hbm)
-    store(low_ref, low_hbm)
     for copy in stores:
         copy.wait()
 
 
-def user_kernel(scales, sizes, x_hbm, y_hbm, high_hbm, low_hbm, keep_ref, send_ref,
-                x_ref, y_ref, high_ref, low_ref, in_sems):
+def user_kernel(scales, sizes, x_hbm, y_hbm, high_ref, low_ref, keep_ref, send_ref,
+                x_ref, y_ref, in_sems):
     user_scale, user_gram, user_ridge = scales
     y_size, core_size = sizes
     item_tiles, _, tile = high_ref.shape
     width = x_ref.shape[1]
-    moves = ((y_hbm, y_ref), (x_hbm, x_ref), (high_hbm, high_ref), (low_hbm, low_ref))
+    moves = ((y_hbm, y_ref), (x_hbm, x_ref))
     loads = [pltpu.make_async_copy(src, dst, in_sems.at[k]) for k, (src, dst) in enumerate(moves)]
     for load in loads:
         load.start()
@@ -178,11 +172,11 @@
         lambda *refs: item_kernel(item_scales, user_axes, *refs),
         out_shape=(
             pltpu.HBM((item_rows, feat_width), F32),
-            pltpu.HBM(sums_shape, BF16),
-            pltpu.HBM(sums_shape, BF16),
+            pltpu.VMEM(sums_shape, BF16),
+            pltpu.VMEM(sums_shape, BF16),
         ),
         in_specs=[in_hbm] * 5,
-        out_specs=(in_hbm,) * 3,
+        out_specs=(in_hbm, in_vmem, in_vmem),
         scratch_shapes=[
             pltpu.VMEM(user_factors.shape, BF16),
             pltpu.VMEM(item_factors.shape, BF16),
@@ -191,11 +185,9 @@
             pltpu.SMEM((1, user_tiles), jnp.int32),
             pltpu.VMEM(sums_shape, F32),
             pltpu.VMEM(sums_shape, F32),
-            pltpu.VMEM(sums_shape, BF16),
-            pltpu.VMEM(sums_shape, BF16),
             pltpu.VMEM((item_rows, feat_width), F32),
-            pltpu.SemaphoreType.DMA((7 + user_tiles,)),
-            pltpu.SemaphoreType.DMA((2 + 2 * item_tiles,)),
+            pltpu.SemaphoreType.DMA((4 + user_tiles,)),
+            pltpu.SemaphoreType.DMA((2 * item_tiles,)),
         ],
         compiler_params=params,
         name="item_sums",
@@ -204,18 +196,16 @@
     keep, send = pl.pallas_call(
         lambda *refs: user_kernel(user_scales, item_axes, *refs),
         out_shape=(pltpu.VMEM((user_rows // 2, feat_width), F32),) * 2,
-        in_specs=[in_hbm] * 4,
+        in_specs=[in_hbm, in_hbm, in_vmem, in_vmem],
         out_specs=(in_vmem,) * 2,
         scratch_shapes=[
             pltpu.VMEM(user_factors.shape, BF16),
             pltpu.VMEM(item_factors.shape, BF16),
-            pltpu.VMEM(sums_shape, BF16),
-            pltpu.VMEM(sums_shape, BF16),
-            pltpu.SemaphoreType.DMA((4,)),
+            pltpu.SemaphoreType.DMA((2,)),
         ],
         compiler_params=params,
         name="user_sums",
-    )(*pinned(user_factors, item_factors, high, low))
+    )(*pinned(user_factors, item_factors), high, low)
 
     def exchange(part, axes):
         size = lax.axis_size(axes)

time: 79.2 us -> 80 us (1.010)
  other arithmetic: 2.12 us -> 3.73 us
  Pallas kernels: 9.46 us -> 8.39 us
    reduce_sum x2, other arithmetic: 1.48 us -> 3.09 us  [shards(): item_gradient = exchange(moved.sum(0), 'zh').sum(0)]
    pallas_call x1, Pallas kernels: 5.75 us -> 4.7 us  [shards(): pl.pallas_call(lambda *refs: item_kernel(item_scales, user_axes, *refs),...]
where the time goes in v5:
time: 80 us; the launch traced here: 79.5 us
  starting transfers between devices  37.9 us (47%)
  waiting for transfers between devices  28.7 us (36%)
  Pallas kernels  8.39 us (10%)
  other arithmetic  3.73 us (5%)
    all_to_all x2, starting transfers between devices, exchange(): moved = lax.all_to_all(part, axes, 0, 0, tiled=True)  24 us
    all_to_all x2, waiting for transfers between devices, exchange(): moved = lax.all_to_all(part, axes, 0, 0, tiled=True)  17.1 us
    ppermute x4, starting transfers between devices, halve(): whole = keep + lax.ppermute(send, name, pairs)  13.9 us
    ppermute x4, waiting for transfers between devices, halve(): whole = keep + lax.ppermute(send, name, pairs)  11.7 us
    pallas_call x1, Pallas kernels, shards(): pl.pallas_call(lambda *refs: item_kernel(item_scales, user_axes, *refs),...  4.7 us
    pallas_call x1, Pallas kernels, shards(): pl.pallas_call(lambda *refs: user_kernel(user_scales, item_axes, *refs),...  3.69 us
    reduce_sum x2, other arithmetic, shards(): item_gradient = exchange(moved.sum(0), 'zh').sum(0)  3.09 us
  transfers between devices with their start and end apart: 6, of which 6 were waited for; matrix products, arithmetic and copies ran while one was open for 1% of the time, Pallas kernels for 5%

profile of v5, /device:TPU:56, one launch (start us, length us, event | category | flops | bytes accessed | tf_op | source)
XLA Modules:
  0.0 79.5 jit_solution(16276385366881699468)
XLA Ops:
  0.6 4.7 %item_sums.1 = (f32[2048,256]{1,0:T(8,128)}, bf16[16,256,128]{2,1,0:T(8,128)(2,1)S(1)}, bf16[16,256,128]{2,1,0:T(8,128)(2,1)S(1)}) custom-call(bf16[256,256]{1,0:T(8,128)(2,1)} %refs_0_.3, bf16[2048,256]{1,0:T(8,128)(2,1)} %refs_1_.3, bf16[2,1,16,128,128]{4,3,2,1,0:T(8,128)(2,1)} %refs_2_.1, s32[2,1,16]{2,1,0:T(1,128)} %refs_3_.1, s32[1,2]{1,0:T(1,128)} %bitcast.6), custom_call_target="tpu_custom_call" | custom-call | tf_op jit(solution)/shard_map/item_sums/pallas_call | solution.py:171
  5.3 6.1 %all-to-all-start = ((f32[8,256,256]{2,1,0:T(8,128)}), f32[8,256,256]{2,1,0:T(8,128)}, u32[]{:S(2)}, u32[]{:S(2)}) async-start(f32[8,256,256]{2,1,0:T(8,128)} %bitcast.4), calls=%async_computation | async-start | bytes 4194304 | tf_op jit(solution)/shard_map/all_to_all | solution.py:212
  11.5 3.7 %user_sums.1 = (f32[128,256]{1,0:T(8,128)S(1)}, f32[128,256]{1,0:T(8,128)S(1)}) custom-call(bf16[256,256]{1,0:T(8,128)(2,1)} %refs_0_.3, bf16[2048,256]{1,0:T(8,128)(2,1)} %refs_1_.3, bf16[16,256,128]{2,1,0:T(8,128)(2,1)S(1)} %get-tuple-element.11.refs_2_, bf16[16,256,128]{2,1,0:T(8,128)(2,1)S(1)} %get-tuple-element.12.refs_3_), custom_call_target="tpu_custom_call" | custom-call | tf_op jit(solution)/shard_map/user_sums/pallas_call | solution.py:196
  15.2 1.9 %collective-permute-start = (f32[128,256]{1,0:T(8,128)S(1)}, f32[128,256]{1,0:T(8,128)S(1)}, u32[]{:S(2)}, u32[]{:S(2)}) collective-permute-start(f32[128,256]{1,0:T(8,128)S(1)} %get-tuple-element.14), channel_id=1, source_target_pairs={{0,1},{1,0},{2,3},{3,2},{4,5},{5,4},{6,7},{7,6},{8,9},{9,8},{10,11... | collective-permute-start | bytes 393224 | tf_op jit(solution)/shard_map/ppermute | solution.py:217
  17.1 1.3 %collective-permute-done = f32[128,256]{1,0:T(8,128)S(1)} collective-permute-done((f32[128,256]{1,0:T(8,128)S(1)}, f32[128,256]{1,0:T(8,128)S(1)}, u32[]{:S(2)}, u32[]{:S(2)}) %collective-permute-start) | collective-permute-done | bytes 131104 | tf_op jit(solution)/shard_map/ppermute | solution.py:217
  18.4 3.3 %collective-permute-start.1 = (f32[64,256]{1,0:T(8,128)S(1)}, f32[64,256]{1,0:T(8,128)S(1)}, u32[]{:S(2)}, u32[]{:S(2)}) collective-permute-start(f32[64,256]{1,0:T(8,128)S(1)} %slice.25), channel_id=1, source_target_pairs={{0,2},{2,0},{4,6},{6,4},{8,10},{10,8},{12,14},{14,12},{1,3},{3,1},... | collective-permute-start | bytes 196616 | tf_op jit(solution)/shard_map/ppermute | solution.py:217
  21.7 2.9 %collective-permute-done.1 = f32[64,256]{1,0:T(8,128)S(1)} collective-permute-done((f32[64,256]{1,0:T(8,128)S(1)}, f32[64,256]{1,0:T(8,128)S(1)}, u32[]{:S(2)}, u32[]{:S(2)}) %collective-permute-start.1) | collective-permute-done | bytes 65568 | tf_op jit(solution)/shard_map/ppermute | solution.py:217
  24.6 4.0 %collective-permute-start.2 = (f32[32,256]{1,0:T(8,128)S(1)}, f32[32,256]{1,0:T(8,128)S(1)}, u32[]{:S(2)}, u32[]{:S(2)}) collective-permute-start(f32[32,256]{1,0:T(8,128)S(1)} %slice.27), channel_id=1, source_target_pairs={{0,4},{2,6},{4,0},{6,2},{8,12},{10,14},{12,8},{14,10},{1,5},{3,7},... | collective-permute-start | bytes 98312 | tf_op jit(solution)/shard_map/ppermute | solution.py:217
  28.7 2.7 %collective-permute-done.2 = f32[32,256]{1,0:T(8,128)S(1)} collective-permute-done((f32[32,256]{1,0:T(8,128)S(1)}, f32[32,256]{1,0:T(8,128)S(1)}, u32[]{:S(2)}, u32[]{:S(2)}) %collective-permute-start.2) | collective-permute-done | bytes 32800 | tf_op jit(solution)/shard_map/ppermute | solution.py:217
  31.3 7.2 %all-to-all-done = f32[8,256,256]{2,1,0:T(8,128)} async-done(((f32[8,256,256]{2,1,0:T(8,128)}), f32[8,256,256]{2,1,0:T(8,128)}, u32[]{:S(2)}, u32[]{:S(2)}) %all-to-all-start) | async-done | bytes 2097184 | tf_op jit(solution)/shard_map/all_to_all | solution.py:212
  38.5 2.5 %reduce_sum.18 = f32[256,256]{1,0:T(8,128)} reduce(f32[8,256,256]{2,1,0:T(8,128)} %all-to-all-done, f32[]{:T(128)} %constant.0.clone.1), dimensions={0}, to_apply=%region_0.0 | reduce | flops 458752 | bytes 2359300 | tf_op jit(solution)/shard_map/reduce_sum | solution.py:226
  41.0 17.9 %all-to-all-start.1 = ((f32[8,32,256]{2,1,0:T(8,128)}), f32[8,32,256]{2,1,0:T(8,128)S(1)}, u32[]{:S(2)}, u32[]{:S(2)}) async-start(f32[8,32,256]{2,1,0:T(8,128)} %bitcast.2), calls=%async_computation.1 | async-start | bytes 524288 | tf_op jit(solution)/shard_map/all_to_all | solution.py:212
  58.9 4.7 %collective-permute-start.3 = (f32[16,256]{1,0:T(8,128)S(1)}, f32[16,256]{1,0:T(8,128)S(1)}, u32[]{:S(2)}, u32[]{:S(2)}) collective-permute-start(f32[16,256]{1,0:T(8,128)S(1)} %get-tuple-element.16), channel_id=1, source_target_pairs={{0,8},{2,10},{4,12},{6,14},{8,0},{10,2},{12,4},{14,6},{1,9},{3,11}... | collective-permute-start | bytes 49160 | tf_op jit(solution)/shard_map/ppermute | solution.py:217
  63.6 4.8 %collective-permute-done.3 = f32[16,256]{1,0:T(8,128)S(1)} collective-permute-done((f32[16,256]{1,0:T(8,128)S(1)}, f32[16,256]{1,0:T(8,128)S(1)}, u32[]{:S(2)}, u32[]{:S(2)}) %collective-permute-start.3) | collective-permute-done | bytes 16416 | tf_op jit(solution)/shard_map/ppermute | solution.py:217
  68.4 0.6 add.15
  69.0 9.9 %all-to-all-done.1 = f32[8,32,256]{2,1,0:T(8,128)S(1)} async-done(((f32[8,32,256]{2,1,0:T(8,128)}), f32[8,32,256]{2,1,0:T(8,128)S(1)}, u32[]{:S(2)}, u32[]{:S(2)}) %all-to-all-start.1) | async-done | bytes 262176 | tf_op jit(solution)/shard_map/all_to_all | solution.py:212
  78.9 0.6 reduce_sum.19
  (6 shorter events, 0.1 us)
Async XLA Ops:
  5.3 33.2 %all-to-all-start = ((f32[8,256,256]{2,1,0:T(8,128)}), f32[8,256,256]{2,1,0:T(8,128)}, u32[]{:S(2)}, u32[]{:S(2)}) async-start(f32[8,256,256]{2,1,0:T(8,128)} %bitcast.4), calls=%async_computation | async-start | bytes 4194304 | tf_op jit(solution)/shard_map/all_to_all | solution.py:212
  15.2 3.2 %collective-permute-start = (f32[128,256]{1,0:T(8,128)S(1)}, f32[128,256]{1,0:T(8,128)S(1)}, u32[]{:S(2)}, u32[]{:S(2)}) collective-permute-start(f32[128,256]{1,0:T(8,128)S(1)} %get-tuple-element.14), channel_id=1, source_target_pairs={{0,1},{1,0},{2,3},{3,2},{4,5},{5,4},{6,7},{7,6},{8,9},{9,8},{10,11... | collective-permute-start | bytes 393224 | tf_op jit(solution)/shard_map/ppermute | solution.py:217
  18.4 6.2 %collective-permute-start.1 = (f32[64,256]{1,0:T(8,128)S(1)}, f32[64,256]{1,0:T(8,128)S(1)}, u32[]{:S(2)}, u32[]{:S(2)}) collective-permute-start(f32[64,256]{1,0:T(8,128)S(1)} %slice.25), channel_id=1, source_target_pairs={{0,2},{2,0},{4,6},{6,4},{8,10},{10,8},{12,14},{14,12},{1,3},{3,1},... | collective-permute-start | bytes 196616 | tf_op jit(solution)/shard_map/ppermute | solution.py:217
  24.6 6.7 %collective-permute-start.2 = (f32[32,256]{1,0:T(8,128)S(1)}, f32[32,256]{1,0:T(8,128)S(1)}, u32[]{:S(2)}, u32[]{:S(2)}) collective-permute-start(f32[32,256]{1,0:T(8,128)S(1)} %slice.27), channel_id=1, source_target_pairs={{0,4},{2,6},{4,0},{6,2},{8,12},{10,14},{12,8},{14,10},{1,5},{3,7},... | collective-permute-start | bytes 98312 | tf_op jit(solution)/shard_map/ppermute | solution.py:217
  41.0 37.8 %all-to-all-start.1 = ((f32[8,32,256]{2,1,0:T(8,128)}), f32[8,32,256]{2,1,0:T(8,128)S(1)}, u32[]{:S(2)}, u32[]{:S(2)}) async-start(f32[8,32,256]{2,1,0:T(8,128)} %bitcast.2), calls=%async_computation.1 | async-start | bytes 524288 | tf_op jit(solution)/shard_map/all_to_all | solution.py:212
  58.9 9.5 %collective-permute-start.3 = (f32[16,256]{1,0:T(8,128)S(1)}, f32[16,256]{1,0:T(8,128)S(1)}, u32[]{:S(2)}, u32[]{:S(2)}) collective-permute-start(f32[16,256]{1,0:T(8,128)S(1)} %get-tuple-element.16), channel_id=1, source_target_pairs={{0,8},{2,10},{4,12},{6,14},{8,0},{10,2},{12,4},{14,6},{1,9},{3,11}... | collective-permute-start | bytes 49160 | tf_op jit(solution)/shard_map/ppermute | solution.py:217

commit v6 on v5

--- a/solution.py
+++ b/solution.py
@@ -30,27 +30,19 @@
     return jnp.where(row == col, value, 0.0).astype(F32)
 
 
-def item_kernel(scales, sizes, x_hbm, y_hbm, c_hbm, pat_hbm, cnt_hbm, item_hbm, high_ref, low_ref,
-                x_ref, y_ref, c_ref, pat, cnt, s_ref, w_ref, item_ref, in_sems, out_sems):
-    item_scale, item_gram, item_ridge = scales
-    x_size, zh_size, zl_size = sizes
+def residual_sums(x_hbm, y_hbm, c_hbm, pat_hbm, cnt_hbm, x_ref, y_ref, c_ref, pat, cnt, s_ref, w_ref, sems, during):
     user_tiles, _, slots, tile, _ = c_ref.shape
-    width = x_ref.shape[1]
-    item_rows = y_ref.shape[0]
-    item_tiles = item_rows // tile
-    owner_rows = item_rows // (x_size * zh_size * zl_size)
-    block = min(tile, owner_rows)
     moves = [(x_hbm, x_ref), (pat_hbm, pat), (cnt_hbm, cnt), (y_hbm, y_ref)]
     moves += [(c_hbm.at[b], c_ref.at[b]) for b in range(user_tiles)]
-    loads = [pltpu.make_async_copy(src, dst, in_sems.at[k]) for k, (src, dst) in enumerate(moves)]
+    loads = [pltpu.make_async_copy(src, dst, sems.at[k]) for k, (src, dst) in enumerate(moves)]
     for load in loads:
         load.start()
     w_ref[...] = jnp.zeros_like(w_ref)
     loads[0].wait()
     x = x_ref[...]
-    gx_high, gx_low = split(dot(x, x, ((0,), (0,))) * item_gram + eye(width, item_ridge))
+    early = during(x)
     loads[3].wait()
-    for t in range(item_tiles):
+    for t in range(w_ref.shape[0]):
         s_ref[t] = dot(x, y_ref[t * tile:(t + 1) * tile, :], ((1,), (1,))) - 1.0
     loads[1].wait()
     loads[2].wait()
@@ -62,6 +54,26 @@
             live = jnp.where(s < cnt[0, b], 1.0, 0.0).astype(F32)
             residual = (live * c_ref[b, 0, s].astype(F32) * s_ref[t, rows, :]).astype(BF16)
             w_ref[t, rows, :] += residual.astype(F32)
+    return early
+
+
+def item_kernel(scales, sizes, x_hbm, y_hbm, c_hbm, pat_hbm, cnt_hbm, item_hbm,
+                x_ref, y_ref, c_ref, pat, cnt, s_ref, w_ref, in_sems, item_ref, out_sems):
+    item_scale, item_gram, item_ridge = scales
+    x_size, zh_size, zl_size = sizes
+    tile = c_ref.shape[-1]
+    width = x_ref.shape[1]
+    item_rows = y_ref.shape[0]
+    item_tiles = item_rows // tile
+    owner_rows = item_rows // (x_size * zh_size * zl_size)
+    block = min(tile, owner_rows)
+
+    def own_gram(x):
+        return split(dot(x, x, ((0,), (0,))) * item_gram + eye(width, item_ridge))
+
+    gx_high, gx_low = residual_sums(
+        x_hbm, y_hbm, c_hbm, pat_hbm, cnt_hbm, x_ref, y_ref, c_ref, pat, cnt, s_ref, w_ref, in_sems, own_gram)
+    x = x_ref[...]
     stores = []
 
     def store(src, dst):
@@ -72,8 +84,6 @@
     for t in range(item_tiles):
         y_t = y_ref[t * tile:(t + 1) * tile, :]
         high, low = split(w_ref[t])
-        high_ref[t] = high
-        low_ref[t] = low
         part = dot(high, x, ((0,), (0,))) + dot(low, x, ((0,), (0,)))
         gram = dot(y_t, gx_high, ((1,), (0,))) + dot(y_t, gx_low, ((1,), (0,)))
         whole = part * item_scale + gram
@@ -95,26 +105,22 @@
         copy.wait()
 
 
-def user_kernel(scales, sizes, x_hbm, y_hbm, high_ref, low_ref, keep_ref, send_ref,
-                x_ref, y_ref, in_sems):
+def user_kernel(scales, sizes, x_hbm, y_hbm, c_hbm, pat_hbm, cnt_hbm, keep_ref, send_ref,
+                x_ref, y_ref, c_ref, pat, cnt, s_ref, w_ref, in_sems):
     user_scale, user_gram, user_ridge = scales
     y_size, core_size = sizes
-    item_tiles, _, tile = high_ref.shape
+    tile = c_ref.shape[-1]
     width = x_ref.shape[1]
-    moves = ((y_hbm, y_ref), (x_hbm, x_ref))
-    loads = [pltpu.make_async_copy(src, dst, in_sems.at[k]) for k, (src, dst) in enumerate(moves)]
-    for load in loads:
-        load.start()
-    loads[0].wait()
+    residual_sums(
+        x_hbm, y_hbm, c_hbm, pat_hbm, cnt_hbm, x_ref, y_ref, c_ref, pat, cnt, s_ref, w_ref, in_sems, lambda x: None)
+    x = x_ref[...]
     y = y_ref[...]
     gy_high, gy_low = split(dot(y, y, ((0,), (0,))) * user_gram + eye(width, user_ridge))
-    for load in loads[1:]:
-        load.wait()
-    x = x_ref[...]
     user = jnp.zeros(x_ref.shape, F32)
-    for t in range(item_tiles):
+    for t in range(w_ref.shape[0]):
         y_t = y_ref[t * tile:(t + 1) * tile, :]
-        user += dot(high_ref[t], y_t, ((1,), (0,))) + dot(low_ref[t], y_t, ((1,), (0,)))
+        high, low = split(w_ref[t])
+        user += dot(high, y_t, ((1,), (0,))) + dot(low, y_t, ((1,), (0,)))
     gram = dot(x, gy_high, ((1,), (0,))) + dot(x, gy_low, ((1,), (0,)))
     user = user * user_scale + gram
     half = keep_ref.shape[0]
@@ -168,44 +174,40 @@
     def pinned(*arrays):
         return [pltpu.with_memory_space_constraint(a, pltpu.HBM) for a in arrays]
 
-    item_part, high, low = pl.pallas_call(
+    operands = pinned(user_factors, item_factors, confidence, pattern, counts.T)
+    scratch = [
+        pltpu.VMEM(user_factors.shape, BF16),
+        pltpu.VMEM(item_factors.shape, BF16),
+        pltpu.VMEM(confidence.shape, BF16),
+        pltpu.SMEM(pattern.shape, jnp.int32),
+        pltpu.SMEM((1, user_tiles), jnp.int32),
+        pltpu.VMEM(sums_shape, F32),
+        pltpu.VMEM(sums_shape, F32),
+        pltpu.SemaphoreType.DMA((4 + user_tiles,)),
+    ]
+
+    item_part = pl.pallas_call(
         lambda *refs: item_kernel(item_scales, user_axes, *refs),
-        out_shape=(
-            pltpu.HBM((item_rows, feat_width), F32),
-            pltpu.VMEM(sums_shape, BF16),
-            pltpu.VMEM(sums_shape, BF16),
-        ),
+        out_shape=pltpu.HBM((item_rows, feat_width), F32),
         in_specs=[in_hbm] * 5,
-        out_specs=(in_hbm, in_vmem, in_vmem),
-        scratch_shapes=[
-            pltpu.VMEM(user_factors.shape, BF16),
-            pltpu.VMEM(item_factors.shape, BF16),
-            pltpu.VMEM(confidence.shape, BF16),
-            pltpu.SMEM(pattern.shape, jnp.int32),
-            pltpu.SMEM((1, user_tiles), jnp.int32),
-            pltpu.VMEM(sums_shape, F32),
-            pltpu.VMEM(sums_shape, F32),
+        out_specs=in_hbm,
+        scratch_shapes=scratch + [
             pltpu.VMEM((item_rows, feat_width), F32),
-            pltpu.SemaphoreType.DMA((4 + user_tiles,)),
             pltpu.SemaphoreType.DMA((2 * item_tiles,)),
         ],
         compiler_params=params,
         name="item_sums",
-    )(*pinned(user_factors, item_factors, confidence, pattern, counts.T))
+    )(*operands)
 
     keep, send = pl.pallas_call(
         lambda *refs: user_kernel(user_scales, item_axes, *refs),
         out_shape=(pltpu.VMEM((user_rows // 2, feat_width), F32),) * 2,
-        in_specs=[in_hbm, in_hbm, in_vmem, in_vmem],
+        in_specs=[in_hbm] * 5,
         out_specs=(in_vmem,) * 2,
-        scratch_shapes=[
-            pltpu.VMEM(user_factors.shape, BF16),
-            pltpu.VMEM(item_factors.shape, BF16),
-            pltpu.SemaphoreType.DMA((2,)),
-        ],
+        scratch_shapes=scratch,
         compiler_params=params,
         name="user_sums",
-    )(*pinned(user_factors, item_factors), high, low)
+    )(*operands)
 
     def exchange(part, axes):
         size = lax.axis_size(axes)

time: 80 us -> 78.2 us (0.978)
  other arithmetic: 3.73 us -> 2.11 us
  waiting for transfers between devices: 28.7 us -> 27.1 us
  Pallas kernels: 8.39 us -> 9.97 us
    all_to_all x2, waiting for transfers between devices: 17.1 us -> 15.4 us  [exchange(): moved = lax.all_to_all(part, axes, 0, 0, tiled=True)]
    reduce_sum x2, other arithmetic: 3.09 us -> 1.47 us  [shards(): item_gradient = exchange(moved.sum(0), 'zh').sum(0)]
    pallas_call x1, Pallas kernels: 3.69 us -> 5.27 us  [shards(): pl.pallas_call(lambda *refs: user_kernel(user_scales, item_axes, *refs),...]
  transfers between devices with their start and end apart: 6 -> 6, of which waited for: 6 -> 6; matrix products, arithmetic and copies ran while one was open for 1% -> 1% of each run, Pallas kernels for 5% -> 7%
where the time goes in v6:
time: 78.2 us; the launch traced here: 77.8 us
  starting transfers between devices  37.9 us (48%)
  waiting for transfers between devices  27.1 us (35%)
  Pallas kernels  9.97 us (13%)
  other arithmetic  2.11 us (3%)
    all_to_all x2, starting transfers between devices, exchange(): moved = lax.all_to_all(part, axes, 0, 0, tiled=True)  24 us
    all_to_all x2, waiting for transfers between devices, exchange(): moved = lax.all_to_all(part, axes, 0, 0, tiled=True)  15.4 us
    ppermute x4, starting transfers between devices, halve(): whole = keep + lax.ppermute(send, name, pairs)  13.9 us
    ppermute x4, waiting for transfers between devices, halve(): whole = keep + lax.ppermute(send, name, pairs)  11.7 us
    pallas_call x1, Pallas kernels, shards(): pl.pallas_call(lambda *refs: user_kernel(user_scales, item_axes, *refs),...  5.27 us
    pallas_call x1, Pallas kernels, shards(): pl.pallas_call(lambda *refs: item_kernel(item_scales, user_axes, *refs),...  4.7 us
  transfers between devices with their start and end apart: 6, of which 6 were waited for; matrix products, arithmetic and copies ran while one was open for 1% of the time, Pallas kernels for 7%

profile of v6, /device:TPU:56, one launch (start us, length us, event | category | flops | bytes accessed | tf_op | source)
XLA Modules:
  0.0 77.8 jit_solution(16287809949242064577)
XLA Ops:
  0.6 4.7 %item_sums.1 = f32[2048,256]{1,0:T(8,128)} custom-call(bf16[256,256]{1,0:T(8,128)(2,1)} %refs_0_.3, bf16[2048,256]{1,0:T(8,128)(2,1)} %refs_1_.3, bf16[2,1,16,128,128]{4,3,2,1,0:T(8,128)(2,1)} %refs_2_.3, s32[2,1,16]{2,1,0:T(1,128)} %refs_3_.3, s32[1,2]{1,0:T(1,128)} %bitcast.6), custom_call_target="tpu_custom_call" | custom-call | tf_op jit(solution)/shard_map/item_sums/pallas_call | solution.py:189
  5.3 6.1 %all-to-all-start = ((f32[8,256,256]{2,1,0:T(8,128)}), f32[8,256,256]{2,1,0:T(8,128)S(1)}, u32[]{:S(2)}, u32[]{:S(2)}) async-start(f32[8,256,256]{2,1,0:T(8,128)} %bitcast.4), calls=%async_computation | async-start | bytes 4194304 | tf_op jit(solution)/shard_map/all_to_all | solution.py:214
  11.5 5.3 %user_sums.1 = (f32[128,256]{1,0:T(8,128)S(1)}, f32[128,256]{1,0:T(8,128)S(1)}) custom-call(bf16[256,256]{1,0:T(8,128)(2,1)} %refs_0_.3, bf16[2048,256]{1,0:T(8,128)(2,1)} %refs_1_.3, bf16[2,1,16,128,128]{4,3,2,1,0:T(8,128)(2,1)} %refs_2_.3, s32[2,1,16]{2,1,0:T(1,128)} %refs_3_.3, s32[1,2]{1,0:T(1,128)} %bitcast.7), custom_call_target="tpu_custom_call" | custom-call | tf_op jit(solution)/shard_map/user_sums/pallas_call | solution.py:202
  16.7 1.9 %collective-permute-start = (f32[128,256]{1,0:T(8,128)S(1)}, f32[128,256]{1,0:T(8,128)S(1)}, u32[]{:S(2)}, u32[]{:S(2)}) collective-permute-start(f32[128,256]{1,0:T(8,128)S(1)} %get-tuple-element.8), channel_id=1, source_target_pairs={{0,1},{1,0},{2,3},{3,2},{4,5},{5,4},{6,7},{7,6},{8,9},{9,8},{10,11... | collective-permute-start | bytes 393224 | tf_op jit(solution)/shard_map/ppermute | solution.py:219
  18.7 1.3 %collective-permute-done = f32[128,256]{1,0:T(8,128)S(1)} collective-permute-done((f32[128,256]{1,0:T(8,128)S(1)}, f32[128,256]{1,0:T(8,128)S(1)}, u32[]{:S(2)}, u32[]{:S(2)}) %collective-permute-start) | collective-permute-done | bytes 131104 | tf_op jit(solution)/shard_map/ppermute | solution.py:219
  20.0 3.3 %collective-permute-start.1 = (f32[64,256]{1,0:T(8,128)S(1)}, f32[64,256]{1,0:T(8,128)S(1)}, u32[]{:S(2)}, u32[]{:S(2)}) collective-permute-start(f32[64,256]{1,0:T(8,128)S(1)} %slice.25), channel_id=1, source_target_pairs={{0,2},{2,0},{4,6},{6,4},{8,10},{10,8},{12,14},{14,12},{1,3},{3,1},... | collective-permute-start | bytes 196616 | tf_op jit(solution)/shard_map/ppermute | solution.py:219
  23.3 2.9 %collective-permute-done.1 = f32[64,256]{1,0:T(8,128)S(1)} collective-permute-done((f32[64,256]{1,0:T(8,128)S(1)}, f32[64,256]{1,0:T(8,128)S(1)}, u32[]{:S(2)}, u32[]{:S(2)}) %collective-permute-start.1) | collective-permute-done | bytes 65568 | tf_op jit(solution)/shard_map/ppermute | solution.py:219
  26.2 4.0 %collective-permute-start.2 = (f32[32,256]{1,0:T(8,128)S(1)}, f32[32,256]{1,0:T(8,128)S(1)}, u32[]{:S(2)}, u32[]{:S(2)}) collective-permute-start(f32[32,256]{1,0:T(8,128)S(1)} %slice.27), channel_id=1, source_target_pairs={{0,4},{2,6},{4,0},{6,2},{8,12},{10,14},{12,8},{14,10},{1,5},{3,7},... | collective-permute-start | bytes 98312 | tf_op jit(solution)/shard_map/ppermute | solution.py:219
  30.2 2.7 %collective-permute-done.2 = f32[32,256]{1,0:T(8,128)S(1)} collective-permute-done((f32[32,256]{1,0:T(8,128)S(1)}, f32[32,256]{1,0:T(8,128)S(1)}, u32[]{:S(2)}, u32[]{:S(2)}) %collective-permute-start.2) | collective-permute-done | bytes 32800 | tf_op jit(solution)/shard_map/ppermute | solution.py:219
  32.9 5.5 %all-to-all-done = f32[8,256,256]{2,1,0:T(8,128)S(1)} async-done(((f32[8,256,256]{2,1,0:T(8,128)}), f32[8,256,256]{2,1,0:T(8,128)S(1)}, u32[]{:S(2)}, u32[]{:S(2)}) %all-to-all-start) | async-done | bytes 2097184 | tf_op jit(solution)/shard_map/all_to_all | solution.py:214
  38.4 0.8 %reduce_sum.18 = f32[256,256]{1,0:T(8,128)} reduce(f32[8,256,256]{2,1,0:T(8,128)S(1)} %all-to-all-done, f32[]{:T(128)} %constant.0.clone.1), dimensions={0}, to_apply=%region_0.0 | reduce | flops 458752 | bytes 2359300 | tf_op jit(solution)/shard_map/reduce_sum | solution.py:228
  39.3 17.9 %all-to-all-start.1 = ((f32[8,32,256]{2,1,0:T(8,128)}), f32[8,32,256]{2,1,0:T(8,128)S(1)}, u32[]{:S(2)}, u32[]{:S(2)}) async-start(f32[8,32,256]{2,1,0:T(8,128)} %bitcast.2), calls=%async_computation.1 | async-start | bytes 524288 | tf_op jit(solution)/shard_map/all_to_all | solution.py:214
  57.1 4.7 %collective-permute-start.3 = (f32[16,256]{1,0:T(8,128)S(1)}, f32[16,256]{1,0:T(8,128)S(1)}, u32[]{:S(2)}, u32[]{:S(2)}) collective-permute-start(f32[16,256]{1,0:T(8,128)S(1)} %get-tuple-element.10), channel_id=1, source_target_pairs={{0,8},{2,10},{4,12},{6,14},{8,0},{10,2},{12,4},{14,6},{1,9},{3,11}... | collective-permute-start | bytes 49160 | tf_op jit(solution)/shard_map/ppermute | solution.py:219
  61.8 4.8 %collective-permute-done.3 = f32[16,256]{1,0:T(8,128)S(1)} collective-permute-done((f32[16,256]{1,0:T(8,128)S(1)}, f32[16,256]{1,0:T(8,128)S(1)}, u32[]{:S(2)}, u32[]{:S(2)}) %collective-permute-start.3) | collective-permute-done | bytes 16416 | tf_op jit(solution)/shard_map/ppermute | solution.py:219
  66.7 0.6 add.15
  67.3 9.9 %all-to-all-done.1 = f32[8,32,256]{2,1,0:T(8,128)S(1)} async-done(((f32[8,32,256]{2,1,0:T(8,128)}), f32[8,32,256]{2,1,0:T(8,128)S(1)}, u32[]{:S(2)}, u32[]{:S(2)}) %all-to-all-start.1) | async-done | bytes 262176 | tf_op jit(solution)/shard_map/all_to_all | solution.py:214
  77.1 0.6 reduce_sum.19
  (6 shorter events, 0.1 us)
Async XLA Ops:
  5.3 33.1 %all-to-all-start = ((f32[8,256,256]{2,1,0:T(8,128)}), f32[8,256,256]{2,1,0:T(8,128)S(1)}, u32[]{:S(2)}, u32[]{:S(2)}) async-start(f32[8,256,256]{2,1,0:T(8,128)} %bitcast.4), calls=%async_computation | async-start | bytes 4194304 | tf_op jit(solution)/shard_map/all_to_all | solution.py:214
  16.7 3.2 %collective-permute-start = (f32[128,256]{1,0:T(8,128)S(1)}, f32[128,256]{1,0:T(8,128)S(1)}, u32[]{:S(2)}, u32[]{:S(2)}) collective-permute-start(f32[128,256]{1,0:T(8,128)S(1)} %get-tuple-element.8), channel_id=1, source_target_pairs={{0,1},{1,0},{2,3},{3,2},{4,5},{5,4},{6,7},{7,6},{8,9},{9,8},{10,11... | collective-permute-start | bytes 393224 | tf_op jit(solution)/shard_map/ppermute | solution.py:219
  20.0 6.2 %collective-permute-start.1 = (f32[64,256]{1,0:T(8,128)S(1)}, f32[64,256]{1,0:T(8,128)S(1)}, u32[]{:S(2)}, u32[]{:S(2)}) collective-permute-start(f32[64,256]{1,0:T(8,128)S(1)} %slice.25), channel_id=1, source_target_pairs={{0,2},{2,0},{4,6},{6,4},{8,10},{10,8},{12,14},{14,12},{1,3},{3,1},... | collective-permute-start | bytes 196616 | tf_op jit(solution)/shard_map/ppermute | solution.py:219
  26.2 6.7 %collective-permute-start.2 = (f32[32,256]{1,0:T(8,128)S(1)}, f32[32,256]{1,0:T(8,128)S(1)}, u32[]{:S(2)}, u32[]{:S(2)}) collective-permute-start(f32[32,256]{1,0:T(8,128)S(1)} %slice.27), channel_id=1, source_target_pairs={{0,4},{2,6},{4,0},{6,2},{8,12},{10,14},{12,8},{14,10},{1,5},{3,7},... | collective-permute-start | bytes 98312 | tf_op jit(solution)/shard_map/ppermute | solution.py:219
  39.3 37.8 %all-to-all-start.1 = ((f32[8,32,256]{2,1,0:T(8,128)}), f32[8,32,256]{2,1,0:T(8,128)S(1)}, u32[]{:S(2)}, u32[]{:S(2)}) async-start(f32[8,32,256]{2,1,0:T(8,128)} %bitcast.2), calls=%async_computation.1 | async-start | bytes 524288 | tf_op jit(solution)/shard_map/all_to_all | solution.py:214
  57.1 9.5 %collective-permute-start.3 = (f32[16,256]{1,0:T(8,128)S(1)}, f32[16,256]{1,0:T(8,128)S(1)}, u32[]{:S(2)}, u32[]{:S(2)}) collective-permute-start(f32[16,256]{1,0:T(8,128)S(1)} %get-tuple-element.10), channel_id=1, source_target_pairs={{0,8},{2,10},{4,12},{6,14},{8,0},{10,2},{12,4},{14,6},{1,9},{3,11}... | collective-permute-start | bytes 49160 | tf_op jit(solution)/shard_map/ppermute | solution.py:219

commit v7 on v6

--- a/solution.py
+++ b/solution.py
@@ -42,8 +42,10 @@
     x = x_ref[...]
     early = during(x)
     loads[3].wait()
-    for t in range(w_ref.shape[0]):
-        s_ref[t] = dot(x, y_ref[t * tile:(t + 1) * tile, :], ((1,), (1,))) - 1.0
+    for t in range(0, w_ref.shape[0], 2):
+        pair = dot(x, y_ref[t * tile:(t + 2) * tile, :], ((1,), (1,))) - 1.0
+        s_ref[t] = pair[:, :tile]
+        s_ref[t + 1] = pair[:, tile:]
     loads[1].wait()
     loads[2].wait()
     for b in range(user_tiles):

time: 78.2 us -> 78 us (level)
  Pallas kernels: 9.97 us -> 9.03 us
  transfers between devices with their start and end apart: 6 -> 6, of which waited for: 6 -> 6; matrix products, arithmetic and copies ran while one was open for 1% -> 1% of each run, Pallas kernels for 7% -> 6%
where the time goes in v7:
time: 78 us; the launch traced here: 77.5 us
  starting transfers between devices  37.9 us (49%)
  waiting for transfers between devices  27.8 us (36%)
  Pallas kernels  9.03 us (12%)
  other arithmetic  2.11 us (3%)
    all_to_all x2, starting transfers between devices, exchange(): moved = lax.all_to_all(part, axes, 0, 0, tiled=True)  24 us
    all_to_all x2, waiting for transfers between devices, exchange(): moved = lax.all_to_all(part, axes, 0, 0, tiled=True)  16.1 us
    ppermute x4, starting transfers between devices, halve(): whole = keep + lax.ppermute(send, name, pairs)  13.9 us
    ppermute x4, waiting for transfers between devices, halve(): whole = keep + lax.ppermute(send, name, pairs)  11.7 us
    pallas_call x1, Pallas kernels, shards(): pl.pallas_call(lambda *refs: user_kernel(user_scales, item_axes, *refs),...  4.55 us
    pallas_call x1, Pallas kernels, shards(): pl.pallas_call(lambda *refs: item_kernel(item_scales, user_axes, *refs),...  4.48 us
  transfers between devices with their start and end apart: 6, of which 6 were waited for; matrix products, arithmetic and copies ran while one was open for 1% of the time, Pallas kernels for 6%

profile of v7, /device:TPU:56, one launch (start us, length us, event | category | flops | bytes accessed | tf_op | source)
XLA Modules:
  0.0 77.5 jit_solution(8958925386892445219)
XLA Ops:
  0.6 4.5 %item_sums.1 = f32[2048,256]{1,0:T(8,128)} custom-call(bf16[256,256]{1,0:T(8,128)(2,1)} %refs_0_.3, bf16[2048,256]{1,0:T(8,128)(2,1)} %refs_1_.3, bf16[2,1,16,128,128]{4,3,2,1,0:T(8,128)(2,1)} %refs_2_.3, s32[2,1,16]{2,1,0:T(1,128)} %refs_3_.3, s32[1,2]{1,0:T(1,128)} %bitcast.6), custom_call_target="tpu_custom_call" | custom-call | tf_op jit(solution)/shard_map/item_sums/pallas_call | solution.py:191
  5.1 6.1 %all-to-all-start = ((f32[8,256,256]{2,1,0:T(8,128)}), f32[8,256,256]{2,1,0:T(8,128)S(1)}, u32[]{:S(2)}, u32[]{:S(2)}) async-start(f32[8,256,256]{2,1,0:T(8,128)} %bitcast.4), calls=%async_computation | async-start | bytes 4194304 | tf_op jit(solution)/shard_map/all_to_all | solution.py:216
  11.2 4.5 %user_sums.1 = (f32[128,256]{1,0:T(8,128)S(1)}, f32[128,256]{1,0:T(8,128)S(1)}) custom-call(bf16[256,256]{1,0:T(8,128)(2,1)} %refs_0_.3, bf16[2048,256]{1,0:T(8,128)(2,1)} %refs_1_.3, bf16[2,1,16,128,128]{4,3,2,1,0:T(8,128)(2,1)} %refs_2_.3, s32[2,1,16]{2,1,0:T(1,128)} %refs_3_.3, s32[1,2]{1,0:T(1,128)} %bitcast.7), custom_call_target="tpu_custom_call" | custom-call | tf_op jit(solution)/shard_map/user_sums/pallas_call | solution.py:204
  15.8 1.9 %collective-permute-start = (f32[128,256]{1,0:T(8,128)S(1)}, f32[128,256]{1,0:T(8,128)S(1)}, u32[]{:S(2)}, u32[]{:S(2)}) collective-permute-start(f32[128,256]{1,0:T(8,128)S(1)} %get-tuple-element.8), channel_id=1, source_target_pairs={{0,1},{1,0},{2,3},{3,2},{4,5},{5,4},{6,7},{7,6},{8,9},{9,8},{10,11... | collective-permute-start | bytes 393224 | tf_op jit(solution)/shard_map/ppermute | solution.py:221
  17.7 1.3 %collective-permute-done = f32[128,256]{1,0:T(8,128)S(1)} collective-permute-done((f32[128,256]{1,0:T(8,128)S(1)}, f32[128,256]{1,0:T(8,128)S(1)}, u32[]{:S(2)}, u32[]{:S(2)}) %collective-permute-start) | collective-permute-done | bytes 131104 | tf_op jit(solution)/shard_map/ppermute | solution.py:221
  19.1 3.2 %collective-permute-start.1 = (f32[64,256]{1,0:T(8,128)S(1)}, f32[64,256]{1,0:T(8,128)S(1)}, u32[]{:S(2)}, u32[]{:S(2)}) collective-permute-start(f32[64,256]{1,0:T(8,128)S(1)} %slice.25), channel_id=1, source_target_pairs={{0,2},{2,0},{4,6},{6,4},{8,10},{10,8},{12,14},{14,12},{1,3},{3,1},... | collective-permute-start | bytes 196616 | tf_op jit(solution)/shard_map/ppermute | solution.py:221
  22.3 2.9 %collective-permute-done.1 = f32[64,256]{1,0:T(8,128)S(1)} collective-permute-done((f32[64,256]{1,0:T(8,128)S(1)}, f32[64,256]{1,0:T(8,128)S(1)}, u32[]{:S(2)}, u32[]{:S(2)}) %collective-permute-start.1) | collective-permute-done | bytes 65568 | tf_op jit(solution)/shard_map/ppermute | solution.py:221
  25.3 4.0 %collective-permute-start.2 = (f32[32,256]{1,0:T(8,128)S(1)}, f32[32,256]{1,0:T(8,128)S(1)}, u32[]{:S(2)}, u32[]{:S(2)}) collective-permute-start(f32[32,256]{1,0:T(8,128)S(1)} %slice.27), channel_id=1, source_target_pairs={{0,4},{2,6},{4,0},{6,2},{8,12},{10,14},{12,8},{14,10},{1,5},{3,7},... | collective-permute-start | bytes 98312 | tf_op jit(solution)/shard_map/ppermute | solution.py:221
  29.3 2.7 %collective-permute-done.2 = f32[32,256]{1,0:T(8,128)S(1)} collective-permute-done((f32[32,256]{1,0:T(8,128)S(1)}, f32[32,256]{1,0:T(8,128)S(1)}, u32[]{:S(2)}, u32[]{:S(2)}) %collective-permute-start.2) | collective-permute-done | bytes 32800 | tf_op jit(solution)/shard_map/ppermute | solution.py:221
  32.0 6.2 %all-to-all-done = f32[8,256,256]{2,1,0:T(8,128)S(1)} async-done(((f32[8,256,256]{2,1,0:T(8,128)}), f32[8,256,256]{2,1,0:T(8,128)S(1)}, u32[]{:S(2)}, u32[]{:S(2)}) %all-to-all-start) | async-done | bytes 2097184 | tf_op jit(solution)/shard_map/all_to_all | solution.py:216
  38.2 0.8 %reduce_sum.18 = f32[256,256]{1,0:T(8,128)} reduce(f32[8,256,256]{2,1,0:T(8,128)S(1)} %all-to-all-done, f32[]{:T(128)} %constant.0.clone.1), dimensions={0}, to_apply=%region_0.0 | reduce | flops 458752 | bytes 2359300 | tf_op jit(solution)/shard_map/reduce_sum | solution.py:230
  39.1 17.9 %all-to-all-start.1 = ((f32[8,32,256]{2,1,0:T(8,128)}), f32[8,32,256]{2,1,0:T(8,128)S(1)}, u32[]{:S(2)}, u32[]{:S(2)}) async-start(f32[8,32,256]{2,1,0:T(8,128)} %bitcast.2), calls=%async_computation.1 | async-start | bytes 524288 | tf_op jit(solution)/shard_map/all_to_all | solution.py:216
  56.9 4.7 %collective-permute-start.3 = (f32[16,256]{1,0:T(8,128)S(1)}, f32[16,256]{1,0:T(8,128)S(1)}, u32[]{:S(2)}, u32[]{:S(2)}) collective-permute-start(f32[16,256]{1,0:T(8,128)S(1)} %get-tuple-element.10), channel_id=1, source_target_pairs={{0,8},{2,10},{4,12},{6,14},{8,0},{10,2},{12,4},{14,6},{1,9},{3,11}... | collective-permute-start | bytes 49160 | tf_op jit(solution)/shard_map/ppermute | solution.py:221
  61.6 4.8 %collective-permute-done.3 = f32[16,256]{1,0:T(8,128)S(1)} collective-permute-done((f32[16,256]{1,0:T(8,128)S(1)}, f32[16,256]{1,0:T(8,128)S(1)}, u32[]{:S(2)}, u32[]{:S(2)}) %collective-permute-start.3) | collective-permute-done | bytes 16416 | tf_op jit(solution)/shard_map/ppermute | solution.py:221
  66.4 0.6 add.15
  67.0 9.9 %all-to-all-done.1 = f32[8,32,256]{2,1,0:T(8,128)S(1)} async-done(((f32[8,32,256]{2,1,0:T(8,128)}), f32[8,32,256]{2,1,0:T(8,128)S(1)}, u32[]{:S(2)}, u32[]{:S(2)}) %all-to-all-start.1) | async-done | bytes 262176 | tf_op jit(solution)/shard_map/all_to_all | solution.py:216
  76.9 0.6 reduce_sum.19
  (6 shorter events, 0.1 us)
Async XLA Ops:
  5.1 33.1 %all-to-all-start = ((f32[8,256,256]{2,1,0:T(8,128)}), f32[8,256,256]{2,1,0:T(8,128)S(1)}, u32[]{:S(2)}, u32[]{:S(2)}) async-start(f32[8,256,256]{2,1,0:T(8,128)} %bitcast.4), calls=%async_computation | async-start | bytes 4194304 | tf_op jit(solution)/shard_map/all_to_all | solution.py:216
  15.8 3.2 %collective-permute-start = (f32[128,256]{1,0:T(8,128)S(1)}, f32[128,256]{1,0:T(8,128)S(1)}, u32[]{:S(2)}, u32[]{:S(2)}) collective-permute-start(f32[128,256]{1,0:T(8,128)S(1)} %get-tuple-element.8), channel_id=1, source_target_pairs={{0,1},{1,0},{2,3},{3,2},{4,5},{5,4},{6,7},{7,6},{8,9},{9,8},{10,11... | collective-permute-start | bytes 393224 | tf_op jit(solution)/shard_map/ppermute | solution.py:221
  19.1 6.2 %collective-permute-start.1 = (f32[64,256]{1,0:T(8,128)S(1)}, f32[64,256]{1,0:T(8,128)S(1)}, u32[]{:S(2)}, u32[]{:S(2)}) collective-permute-start(f32[64,256]{1,0:T(8,128)S(1)} %slice.25), channel_id=1, source_target_pairs={{0,2},{2,0},{4,6},{6,4},{8,10},{10,8},{12,14},{14,12},{1,3},{3,1},... | collective-permute-start | bytes 196616 | tf_op jit(solution)/shard_map/ppermute | solution.py:221
  25.3 6.7 %collective-permute-start.2 = (f32[32,256]{1,0:T(8,128)S(1)}, f32[32,256]{1,0:T(8,128)S(1)}, u32[]{:S(2)}, u32[]{:S(2)}) collective-permute-start(f32[32,256]{1,0:T(8,128)S(1)} %slice.27), channel_id=1, source_target_pairs={{0,4},{2,6},{4,0},{6,2},{8,12},{10,14},{12,8},{14,10},{1,5},{3,7},... | collective-permute-start | bytes 98312 | tf_op jit(solution)/shard_map/ppermute | solution.py:221
  39.1 37.8 %all-to-all-start.1 = ((f32[8,32,256]{2,1,0:T(8,128)}), f32[8,32,256]{2,1,0:T(8,128)S(1)}, u32[]{:S(2)}, u32[]{:S(2)}) async-start(f32[8,32,256]{2,1,0:T(8,128)} %bitcast.2), calls=%async_computation.1 | async-start | bytes 524288 | tf_op jit(solution)/shard_map/all_to_all | solution.py:216
  56.9 9.5 %collective-permute-start.3 = (f32[16,256]{1,0:T(8,128)S(1)}, f32[16,256]{1,0:T(8,128)S(1)}, u32[]{:S(2)}, u32[]{:S(2)}) collective-permute-start(f32[16,256]{1,0:T(8,128)S(1)} %get-tuple-element.10), channel_id=1, source_target_pairs={{0,8},{2,10},{4,12},{6,14},{8,0},{10,2},{12,4},{14,6},{1,9},{3,11}... | collective-permute-start | bytes 49160 | tf_op jit(solution)/shard_map/ppermute | solution.py:221
